TPU v7x, 128 devices: a whole 4x4x4 slice. The times are simulated.
128 devices in a mesh: atoms: 64 (over y_hi, x, z, core), dirs: 2 (over y_lo).
Axes of the slice: x: 4, y: 4 (y_hi: 2, y_lo: 2; y = y_hi * 2 + y_lo), z: 4, core: 2. Of those that a mesh axis runs over, the one named last changes fastest.
Arguments:
- queries: bfloat16 [131072, 128], P('atoms'), may hold values from -6 to 6
- keys: bfloat16 [131072, 128], P('atoms'), may hold values from -6 to 6
- values: bfloat16 [131072, 128], P('atoms'), may hold values from -6 to 6
- cotangent: bfloat16 [131072, 128], P('atoms'), may hold values from -6 to 6
- positions: float32 [3, 131072], P(None, 'atoms'), may hold values from -128 to 128
- species: int32 [131072], P('atoms'), may hold values from 0 to 4
- domain: int32 [131072], P('atoms'), may hold values from 0 to 64, as said below
- species_gain: float32 [5, 128], replicated, may hold values from 0.1 to 1.9
- frequency: float32 [32], replicated, may hold values from 0.02 to 1
- directions: float32 [3, 88], P(None, 'dirs'), may hold values from -1 to 1, as said below
- dir_weight: float32 [88], P('dirs'), may hold values from 0.003 to 0.03
- dir_mask: int32 [88], P('dirs'), may hold values from 0 to 1, as said below
Outputs:
- attended: bfloat16 [131072, 128], P(('atoms', 'dirs'))
- grad_queries: bfloat16 [131072, 128], P(('atoms', 'dirs'))
- grad_keys: bfloat16 [131072, 128], P(('atoms', 'dirs'))
- grad_values: bfloat16 [131072, 128], P(('atoms', 'dirs'))
Inputs may be any that keep to these rules, and one draw needn't show every extreme that they name: The 2048 slots from b * 2048 on belong to domain b: they hold b for its atoms first, then 131072 // 2048 for empty slots; every domain has 1024 to 2048 atoms. `directions`: each column is a unit vector. `dir_mask`: exactly 86 entries are 1.
All inputs are finite; a program needn't handle non-finite values.
Results may differ from a plain program's by a relative error of at most 0.012.
Values may be sent and summed in bfloat16 or wider, within the bound.
A program may use at most 128 MiB of HBM per device.

v0:
```python
import math

import jax
import jax.numpy as jnp
from jax import lax
from jax.sharding import PartitionSpec as P


def rotate(features, cosine, sine_val):
    half_width = features.shape[-1] // 2
    leading = features[..., :half_width]
    trailing = features[..., half_width:]
    return jnp.concatenate(
        [leading * cosine - trailing * sine_val, leading * sine_val + trailing * cosine], axis=-1
    )


def phases(dir_proj, pair_freq):
    phase_angle = dir_proj[..., None] * pair_freq
    return (jnp.cos(phase_angle), jnp.sin(phase_angle))


def sum_states(states):
    return lax.psum(states, "atoms").astype(jnp.bfloat16)


def sum_grads(state_grads):
    return lax.psum(state_grads, "atoms").astype(jnp.bfloat16)


def per_device(
    queries,
    keys,
    values,
    cotangent,
    positions,
    species,
    domain,
    species_gain,
    frequency,
    directions,
    dir_weight,
    dir_mask,
):
    atom_count = queries.shape[0]
    feat_width = queries.shape[1]
    local_dirs = dir_weight.shape[0]
    group_size = 4
    group_count = local_dirs // group_size
    alive_mask = (domain == lax.axis_index("atoms")).astype(jnp.float32)[:, None]
    species_ids = jnp.arange(species_gain.shape[0], dtype=jnp.int32)
    chosen = (species[:, None] == species_ids[None, :]).astype(jnp.float32)
    gain_rows = jnp.sum(chosen[:, :, None] * species_gain[None, :, :], axis=1)
    keys_gained = keys.astype(jnp.float32) * gain_rows * alive_mask
    queries_full = queries.astype(jnp.float32)
    alive_half = alive_mask.astype(jnp.bfloat16)
    values_live = values * alive_half
    grad_live = cotangent * alive_half
    pair_freq = jnp.tile(frequency, feat_width // 2 // frequency.shape[0])
    projected = (
        directions[0][:, None] * positions[0][None, :]
        + directions[1][:, None] * positions[1][None, :]
    )
    projected = projected + directions[2][:, None] * positions[2][None, :]
    projected = projected.reshape(group_count, group_size, atom_count)
    dir_coef = (
        dir_weight * dir_mask.astype(jnp.float32) / math.sqrt(feat_width * atom_count)
    ).reshape(group_count, group_size)

    def key_states(dir_proj):
        cosine, sine_val = phases(dir_proj, pair_freq)
        key_rot = rotate(keys_gained, cosine, sine_val).astype(jnp.bfloat16)
        return jnp.einsum("gna,nb->gab", key_rot, values_live, preferred_element_type=jnp.float32)

    states = lax.map(key_states, projected)
    states_b = sum_states(states)

    def query_step(totals, inputs_step):
        out_total, query_total = totals
        dir_proj, dir_scale, state_group = inputs_step
        cosine, sine_val = phases(dir_proj, pair_freq)
        query_rot = rotate(queries_full, cosine, sine_val).astype(jnp.bfloat16)
        mixed_rows = jnp.einsum(
            "gna,gab->gnb", query_rot, state_group, preferred_element_type=jnp.float32
        )
        out_total = out_total + jnp.sum(dir_scale[:, None, None] * mixed_rows, axis=0)
        back_proj = jnp.einsum(
            "nb,gab->gna", grad_live, state_group, preferred_element_type=jnp.float32
        )
        query_total = query_total + jnp.sum(
            rotate(dir_scale[:, None, None] * back_proj, cosine, -sine_val), axis=0
        )
        state_grad = dir_scale[:, None, None] * jnp.einsum(
            "gna,nb->gab", query_rot, grad_live, preferred_element_type=jnp.float32
        )
        return ((out_total, query_total), state_grad)

    zeros_full = jnp.zeros((atom_count, feat_width), jnp.float32)
    query_totals, late_grads = lax.scan(
        query_step, (zeros_full, zeros_full), (projected, dir_coef, states_b)
    )
    out_total, query_total = query_totals
    attended = lax.psum_scatter(
        (out_total * alive_mask).astype(jnp.bfloat16), "dirs", scatter_dimension=0, tiled=True
    )
    grads_b = sum_grads(late_grads)

    def key_step(totals, inputs_step):
        key_total, value_total = totals
        dir_proj, grad_group = inputs_step
        cosine, sine_val = phases(dir_proj, pair_freq)
        key_rot = rotate(keys_gained, cosine, sine_val).astype(jnp.bfloat16)
        back_proj = jnp.einsum(
            "nb,gab->gna", values_live, grad_group, preferred_element_type=jnp.float32
        )
        key_total = key_total + jnp.sum(rotate(back_proj, cosine, -sine_val), axis=0)
        value_total = value_total + jnp.einsum(
            "gna,gab->nb", key_rot, grad_group, preferred_element_type=jnp.float32
        )
        return ((key_total, value_total), None)

    key_totals, _ = lax.scan(key_step, (zeros_full, zeros_full), (projected, grads_b))
    key_total, value_total = key_totals
    key_terms = key_total * gain_rows * alive_mask
    grad_queries, grad_keys, grad_values = (
        lax.psum_scatter(
            query_total.astype(jnp.bfloat16), "dirs", scatter_dimension=0, tiled=True
        ).astype(jnp.float32),
        lax.psum_scatter(
            key_terms.astype(jnp.bfloat16), "dirs", scatter_dimension=0, tiled=True
        ).astype(jnp.float32),
        lax.psum_scatter(
            value_total.astype(jnp.bfloat16), "dirs", scatter_dimension=0, tiled=True
        ).astype(jnp.float32),
    )
    return (
        attended,
        grad_queries.astype(jnp.bfloat16),
        grad_keys.astype(jnp.bfloat16),
        grad_values.astype(jnp.bfloat16),
    )


def solution(mesh):
    return jax.shard_map(
        per_device,
        mesh=mesh,
        in_specs=(
            P("atoms", None),
            P("atoms", None),
            P("atoms", None),
            P("atoms", None),
            P(None, "atoms"),
            P("atoms"),
            P("atoms"),
            P(),
            P(),
            P(None, "dirs"),
            P("dirs"),
            P("dirs"),
        ),
        out_specs=(
            P(("atoms", "dirs"), None),
            P(("atoms", "dirs"), None),
            P(("atoms", "dirs"), None),
            P(("atoms", "dirs"), None),
        ),
        check_vma=False,
    )
```

profile of v0, /device:TPU:1, one launch (start us, length us, event | category | flops | bytes accessed | tf_op | source)
XLA Modules:
  0.0 1594.4 jit_solution(8820927007440727935)
XLA Ops:
  20.7 107.1 %while.39 = (s32[]{:T(128)}, f32[11,4,128,128]{3,2,1,0:T(8,128)}, f32[2048,128]{0,1:T(8,128)S(1)}, f32[11,4,2048]{2,1,0:T(4,128)S(1)}, bf16[2048,128]{1,0:T(8,128)(2,1)S(1)}, /*index=5*/f32[32]{0:T(128)S(1)}, s32[]{:T(128)}) while((s32[]{:T(128)}, f32[11,4,128,128]{3,2,1,0:T(8,128)}, f32[2048,128]{0,1:T(8,128)S(1)}, ...), condition=%wide.region_2.3_spmd.clone, body=%wide.region_1.2_spmd.clone.sunk | while | flops 277348352 | bytes 8226513 | solution.py:75
  20.9 8.1 fusion.110
  30.6 8.1 fusion.110
  40.4 8.1 fusion.110
  50.1 8.1 fusion.110
  59.8 8.1 fusion.110
  69.6 8.1 fusion.110
  79.3 8.1 fusion.110
  89.0 8.1 fusion.110
  98.8 8.1 fusion.110
  108.5 8.1 fusion.110
  118.3 8.1 fusion.110
  127.8 355.2 %all-reduce.2 = bf16[11,4,128,128]{3,2,1,0:T(8,128)(2,1)} all-reduce(f32[11,4,128,128]{3,2,1,0:T(8,128)} %get-tuple-element.133), channel_id=1, replica_groups=mesh['atoms'=64,'dirs'=2] {'atoms'}, use_global_device_ids=true, to_apply=%region_3.4 | all-reduce | flops 720896 | bytes 4325376 | tf_op jit(solution)/shard_map/psum | solution.py:24
  485.8 421.8 %while.40 = (s32[]{:T(128)}, f32[2048,128]{1,0:T(8,128)}, f32[2048,128]{1,0:T(8,128)}, f32[11,4,128,128]{3,2,1,0:T(8,128)}, f32[11,4]{1,0:T(8,128)}, /*index=5*/...) while((s32[]{:T(128)}, f32[2048,128]{1,0:T(8,128)}, ...), condition=%wide.region_7.8_spmd.clone, body=%wide.region_4.7_spmd.clone.sunk | while | flops 827916288 | bytes 36278156 | solution.py:99
  486.5 3.9 multiply_bitcast_fusion.2
  493.0 19.9 %fusion.118 = (f32[4,2048,64]{2,1,0:T(8,128)S(1)}, f32[4,2048,64]{2,1,0:T(8,128)S(1)}, bf16[4,2048,64]{2,1,0:T(8,128)(2,1)S(1)}, bf16[4,2048,64]{2,1,0:T(8,128)(2,1)S(1)}) fusion(f32[4,2048,128]{2,1,0:T(8,128)} %multiply_bitcast_fusion.2, f32[64]{0:T(128)S(1)} %mul.663, f32[4,2048]{1,0:T(4,128)S(1)} %dynamic-slice_bitcast_fusion.7, ...), kind=kLoop, calls=%fused_computation.33.clone.1 | loop fusion | flops 8388608 | bytes 11567360 | tf_op jit(solution)/shard_map/while/body/eval_jaxpr/sub | solution.py:14
  524.2 3.9 multiply_bitcast_fusion.2
  530.8 19.9 %fusion.118 = (f32[4,2048,64]{2,1,0:T(8,128)S(1)}, f32[4,2048,64]{2,1,0:T(8,128)S(1)}, bf16[4,2048,64]{2,1,0:T(8,128)(2,1)S(1)}, bf16[4,2048,64]{2,1,0:T(8,128)(2,1)S(1)}) fusion(f32[4,2048,128]{2,1,0:T(8,128)} %multiply_bitcast_fusion.2, f32[64]{0:T(128)S(1)} %mul.663, f32[4,2048]{1,0:T(4,128)S(1)} %dynamic-slice_bitcast_fusion.7, ...), kind=kLoop, calls=%fused_computation.33.clone.1 | loop fusion | flops 8388608 | bytes 11567360 | tf_op jit(solution)/shard_map/while/body/eval_jaxpr/sub | solution.py:14
  562.7 3.9 multiply_bitcast_fusion.2
  569.2 19.9 %fusion.118 = (f32[4,2048,64]{2,1,0:T(8,128)S(1)}, f32[4,2048,64]{2,1,0:T(8,128)S(1)}, bf16[4,2048,64]{2,1,0:T(8,128)(2,1)S(1)}, bf16[4,2048,64]{2,1,0:T(8,128)(2,1)S(1)}) fusion(f32[4,2048,128]{2,1,0:T(8,128)} %multiply_bitcast_fusion.2, f32[64]{0:T(128)S(1)} %mul.663, f32[4,2048]{1,0:T(4,128)S(1)} %dynamic-slice_bitcast_fusion.7, ...), kind=kLoop, calls=%fused_computation.33.clone.1 | loop fusion | flops 8388608 | bytes 11567360 | tf_op jit(solution)/shard_map/while/body/eval_jaxpr/sub | solution.py:14
  601.1 3.9 multiply_bitcast_fusion.2
  607.6 19.9 %fusion.118 = (f32[4,2048,64]{2,1,0:T(8,128)S(1)}, f32[4,2048,64]{2,1,0:T(8,128)S(1)}, bf16[4,2048,64]{2,1,0:T(8,128)(2,1)S(1)}, bf16[4,2048,64]{2,1,0:T(8,128)(2,1)S(1)}) fusion(f32[4,2048,128]{2,1,0:T(8,128)} %multiply_bitcast_fusion.2, f32[64]{0:T(128)S(1)} %mul.663, f32[4,2048]{1,0:T(4,128)S(1)} %dynamic-slice_bitcast_fusion.7, ...), kind=kLoop, calls=%fused_computation.33.clone.1 | loop fusion | flops 8388608 | bytes 11567360 | tf_op jit(solution)/shard_map/while/body/eval_jaxpr/sub | solution.py:14
  639.5 3.9 multiply_bitcast_fusion.2
  646.0 19.9 %fusion.118 = (f32[4,2048,64]{2,1,0:T(8,128)S(1)}, f32[4,2048,64]{2,1,0:T(8,128)S(1)}, bf16[4,2048,64]{2,1,0:T(8,128)(2,1)S(1)}, bf16[4,2048,64]{2,1,0:T(8,128)(2,1)S(1)}) fusion(f32[4,2048,128]{2,1,0:T(8,128)} %multiply_bitcast_fusion.2, f32[64]{0:T(128)S(1)} %mul.663, f32[4,2048]{1,0:T(4,128)S(1)} %dynamic-slice_bitcast_fusion.7, ...), kind=kLoop, calls=%fused_computation.33.clone.1 | loop fusion | flops 8388608 | bytes 11567360 | tf_op jit(solution)/shard_map/while/body/eval_jaxpr/sub | solution.py:14
  677.9 3.9 multiply_bitcast_fusion.2
  684.4 19.9 %fusion.118 = (f32[4,2048,64]{2,1,0:T(8,128)S(1)}, f32[4,2048,64]{2,1,0:T(8,128)S(1)}, bf16[4,2048,64]{2,1,0:T(8,128)(2,1)S(1)}, bf16[4,2048,64]{2,1,0:T(8,128)(2,1)S(1)}) fusion(f32[4,2048,128]{2,1,0:T(8,128)} %multiply_bitcast_fusion.2, f32[64]{0:T(128)S(1)} %mul.663, f32[4,2048]{1,0:T(4,128)S(1)} %dynamic-slice_bitcast_fusion.7, ...), kind=kLoop, calls=%fused_computation.33.clone.1 | loop fusion | flops 8388608 | bytes 11567360 | tf_op jit(solution)/shard_map/while/body/eval_jaxpr/sub | solution.py:14
  716.2 3.9 multiply_bitcast_fusion.2
  722.8 19.9 %fusion.118 = (f32[4,2048,64]{2,1,0:T(8,128)S(1)}, f32[4,2048,64]{2,1,0:T(8,128)S(1)}, bf16[4,2048,64]{2,1,0:T(8,128)(2,1)S(1)}, bf16[4,2048,64]{2,1,0:T(8,128)(2,1)S(1)}) fusion(f32[4,2048,128]{2,1,0:T(8,128)} %multiply_bitcast_fusion.2, f32[64]{0:T(128)S(1)} %mul.663, f32[4,2048]{1,0:T(4,128)S(1)} %dynamic-slice_bitcast_fusion.7, ...), kind=kLoop, calls=%fused_computation.33.clone.1 | loop fusion | flops 8388608 | bytes 11567360 | tf_op jit(solution)/shard_map/while/body/eval_jaxpr/sub | solution.py:14
  754.6 3.9 multiply_bitcast_fusion.2
  761.2 19.9 %fusion.118 = (f32[4,2048,64]{2,1,0:T(8,128)S(1)}, f32[4,2048,64]{2,1,0:T(8,128)S(1)}, bf16[4,2048,64]{2,1,0:T(8,128)(2,1)S(1)}, bf16[4,2048,64]{2,1,0:T(8,128)(2,1)S(1)}) fusion(f32[4,2048,128]{2,1,0:T(8,128)} %multiply_bitcast_fusion.2, f32[64]{0:T(128)S(1)} %mul.663, f32[4,2048]{1,0:T(4,128)S(1)} %dynamic-slice_bitcast_fusion.7, ...), kind=kLoop, calls=%fused_computation.33.clone.1 | loop fusion | flops 8388608 | bytes 11567360 | tf_op jit(solution)/shard_map/while/body/eval_jaxpr/sub | solution.py:14
  793.1 3.9 multiply_bitcast_fusion.2
  799.6 19.9 %fusion.118 = (f32[4,2048,64]{2,1,0:T(8,128)S(1)}, f32[4,2048,64]{2,1,0:T(8,128)S(1)}, bf16[4,2048,64]{2,1,0:T(8,128)(2,1)S(1)}, bf16[4,2048,64]{2,1,0:T(8,128)(2,1)S(1)}) fusion(f32[4,2048,128]{2,1,0:T(8,128)} %multiply_bitcast_fusion.2, f32[64]{0:T(128)S(1)} %mul.663, f32[4,2048]{1,0:T(4,128)S(1)} %dynamic-slice_bitcast_fusion.7, ...), kind=kLoop, calls=%fused_computation.33.clone.1 | loop fusion | flops 8388608 | bytes 11567360 | tf_op jit(solution)/shard_map/while/body/eval_jaxpr/sub | solution.py:14
  831.5 3.9 multiply_bitcast_fusion.2
  838.0 19.9 %fusion.118 = (f32[4,2048,64]{2,1,0:T(8,128)S(1)}, f32[4,2048,64]{2,1,0:T(8,128)S(1)}, bf16[4,2048,64]{2,1,0:T(8,128)(2,1)S(1)}, bf16[4,2048,64]{2,1,0:T(8,128)(2,1)S(1)}) fusion(f32[4,2048,128]{2,1,0:T(8,128)} %multiply_bitcast_fusion.2, f32[64]{0:T(128)S(1)} %mul.663, f32[4,2048]{1,0:T(4,128)S(1)} %dynamic-slice_bitcast_fusion.7, ...), kind=kLoop, calls=%fused_computation.33.clone.1 | loop fusion | flops 8388608 | bytes 11567360 | tf_op jit(solution)/shard_map/while/body/eval_jaxpr/sub | solution.py:14
  869.9 3.9 multiply_bitcast_fusion.2
  876.4 19.9 %fusion.118 = (f32[4,2048,64]{2,1,0:T(8,128)S(1)}, f32[4,2048,64]{2,1,0:T(8,128)S(1)}, bf16[4,2048,64]{2,1,0:T(8,128)(2,1)S(1)}, bf16[4,2048,64]{2,1,0:T(8,128)(2,1)S(1)}) fusion(f32[4,2048,128]{2,1,0:T(8,128)} %multiply_bitcast_fusion.2, f32[64]{0:T(128)S(1)} %mul.663, f32[4,2048]{1,0:T(4,128)S(1)} %dynamic-slice_bitcast_fusion.7, ...), kind=kLoop, calls=%fused_computation.33.clone.1 | loop fusion | flops 8388608 | bytes 11567360 | tf_op jit(solution)/shard_map/while/body/eval_jaxpr/sub | solution.py:14
  907.6 353.0 %all-reduce.3 = bf16[11,4,128,128]{3,2,1,0:T(8,128)(2,1)S(1)} all-reduce(f32[11,4,128,128]{3,2,1,0:T(8,128)} %get-tuple-element.136), channel_id=1, replica_groups=mesh['atoms'=64,'dirs'=2] {'atoms'}, use_global_device_ids=true, to_apply=%region_10.11 | all-reduce | flops 720896 | bytes 4325376 | tf_op jit(solution)/shard_map/psum | solution.py:28
  1260.6 241.8 %while.41 = (s32[]{:T(128)}, f32[2048,128]{0,1:T(8,128)}, f32[2048,128]{1,0:T(8,128)}, bf16[11,4,128,128]{3,2,1,0:T(8,128)(2,1)S(1)}, bf16[2048,128]{1,0:T(8,128...) while((s32[]{:T(128)}, f32[2048,128]{0,1:T(8,128)}, ...), condition=%wide.region_13.14_spmd.clone, body=%wide.region_11.13_spmd.clone.sunk | while | flops 552337408 | bytes 53315436 | solution.py:122
  1264.6 11.5 fusion.125
  1276.0 3.5 fusion.126
  1285.7 11.5 fusion.125
  1297.1 3.8 fusion.126
  1307.8 11.5 fusion.125
  1319.2 3.8 fusion.126
  1329.8 11.5 fusion.125
  1341.3 3.8 fusion.126
  1351.9 11.5 fusion.125
  1363.3 3.8 fusion.126
  1373.9 11.5 fusion.125
  1385.4 3.8 fusion.126
  1396.0 11.5 fusion.125
  1407.5 3.8 fusion.126
  1418.1 11.5 fusion.125
  1429.5 3.8 fusion.126
  1440.1 11.5 fusion.125
  1451.6 3.8 fusion.126
  1462.2 11.5 fusion.125
  1473.7 3.8 fusion.126
  1484.3 11.5 fusion.125
  1495.7 3.8 fusion.126
  1509.4 15.4 reduce-scatter.5.cloned.1.call-done
  1524.8 21.1 %reduce-scatter.9.cloned.1.call-done = bf16[1024,128]{1,0:T(8,128)(2,1)} async-done(((bf16[2048,128]{1,0:T(8,128)(2,1)}), bf16[1024,128]{1,0:T(8,128)(2,1)}) %reduce-scatter.9.cloned.1.call-update) | async-done | bytes 262160 | tf_op jit(solution)/shard_map/reduce_scatter | solution.py:129
  1545.9 21.0 %reduce-scatter.11.cloned.1.call-done = bf16[1024,128]{1,0:T(8,128)(2,1)} async-done(((bf16[2048,128]{1,0:T(8,128)(2,1)}), bf16[1024,128]{1,0:T(8,128)(2,1)}) %reduce-scatter.11.cloned.1.call-update) | async-done | bytes 262160 | tf_op jit(solution)/shard_map/reduce_scatter | solution.py:132
  1566.9 21.0 %reduce-scatter.7.cloned.1.call-done = bf16[1024,128]{1,0:T(8,128)(2,1)} async-done(((bf16[2048,128]{1,0:T(8,128)(2,1)}), bf16[1024,128]{1,0:T(8,128)(2,1)}) %reduce-scatter.7.cloned.1.call-update) | async-done | bytes 262160 | tf_op jit(solution)/shard_map/reduce_scatter | solution.py:126
  (422 shorter events, 273.8 us)
Async XLA Ops:
  7.2 1517.6 %reduce-scatter.5.cloned.1.call-start = ((), (), s32[]{:S(2)}) async-start(), calls=%async_computation.4 | async-start | bytes 786432 | tf_op jit(solution)/shard_map/reduce_scatter | solution.py:103
  127.8 355.2 %copy-start.3 = (bf16[2048,128]{1,0:T(8,128)(2,1)}, bf16[2048,128]{1,0:T(8,128)(2,1)S(1)}, u32[]{:S(2)}) copy-start(bf16[2048,128]{1,0:T(8,128)(2,1)S(1)} %get-tuple-element.633) | copy-start | bytes 1572868
  127.8 355.2 %copy-start.10 = (bf16[2048,128]{1,0:T(8,128)(2,1)S(1)}, bf16[2048,128]{1,0:T(8,128)(2,1)}, u32[]{:S(2)}) copy-start(bf16[2048,128]{1,0:T(8,128)(2,1)} %param.18) | copy-start | bytes 1572868
  127.8 355.3 %copy-start.13 = (f32[44]{0:T(128)S(1)}, f32[44]{0:T(128)}, u32[]{:S(2)}) copy-start(f32[44]{0:T(128)} %param.28) | copy-start | bytes 532
  127.8 355.3 %copy-start.14 = (s32[44]{0:T(128)S(1)}, s32[44]{0:T(128)}, u32[]{:S(2)}) copy-start(s32[44]{0:T(128)} %param.29) | copy-start | bytes 532
  483.0 2.8 copy-start.16
  485.8 5.9 copy-start.17
  520.7 2.8 copy-start.18
  523.6 5.9 copy-start.17
  558.5 3.4 copy-start.18
  562.0 5.9 copy-start.17
  596.9 3.4 copy-start.18
  600.4 5.9 copy-start.17
  635.3 3.4 copy-start.18
  638.8 5.9 copy-start.17
  673.7 3.4 copy-start.18
  677.2 5.9 copy-start.17
  712.1 3.4 copy-start.18
  715.5 5.9 copy-start.17
  750.5 3.4 copy-start.18
  753.9 5.9 copy-start.17
  788.9 3.4 copy-start.18
  792.4 5.9 copy-start.17
  827.4 3.4 copy-start.18
  830.8 5.9 copy-start.17
  865.8 3.4 copy-start.18
  869.2 5.9 copy-start.17
  904.2 3.4 copy-start.18
  907.6 353.0 %copy-start.4 = (bf16[2048,128]{1,0:T(8,128)(2,1)S(1)}, bf16[2048,128]{1,0:T(8,128)(2,1)}, u32[]{:S(2)}) copy-start(bf16[2048,128]{1,0:T(8,128)(2,1)} %copy-done.3) | copy-start | bytes 1572868
  1260.7 2.8 copy-start.8
  1276.0 3.5 copy-start
  1281.8 2.8 copy-start.8
  1297.1 3.8 copy-start
  1301.3 2.5 copy-start.5
  1303.8 2.8 copy-start.8
  1319.2 3.8 copy-start
  1323.4 2.5 copy-start.5
  1325.9 2.8 copy-start.8
  1341.3 3.8 copy-start
  1345.4 2.5 copy-start.5
  1348.0 2.8 copy-start.8
  1363.3 3.8 copy-start
  1367.5 2.5 copy-start.5
  1370.0 2.8 copy-start.8
  1385.4 3.8 copy-start
  1389.6 2.5 copy-start.5
  1392.1 2.8 copy-start.8
  1407.5 3.8 copy-start
  1411.6 2.5 copy-start.5
  1414.1 2.8 copy-start.8
  1429.5 3.8 copy-start
  1433.7 2.5 copy-start.5
  1436.2 2.8 copy-start.8
  1451.6 3.8 copy-start
  1455.8 2.5 copy-start.5
  1458.3 2.8 copy-start.8
  1473.7 3.8 copy-start
  1477.8 2.5 copy-start.5
  1480.3 2.8 copy-start.8
  1495.7 3.8 copy-start
  1505.6 3.0 copy-start.1
  1505.6 40.3 %reduce-scatter.9.cloned.1.call-start = ((), (), s32[]{:S(2)}) async-start(), calls=%async_computation.6 | async-start | bytes 786432 | tf_op jit(solution)/shard_map/reduce_scatter | solution.py:129
  1506.4 60.6 %reduce-scatter.11.cloned.1.call-start = ((), (), s32[]{:S(2)}) async-start(), calls=%async_computation.7 | async-start | bytes 786432 | tf_op jit(solution)/shard_map/reduce_scatter | solution.py:132
  1508.5 79.4 %reduce-scatter.7.cloned.1.call-start = ((), (), s32[]{:S(2)}) async-start(), calls=%async_computation.5 | async-start | bytes 786432 | tf_op jit(solution)/shard_map/reduce_scatter | solution.py:126
  (19 other events, 41.3 us)
Sparse Core Ops, SparseCore 0:
  1505.7 18.9 reduce-scatter.4
  1527.8 18.0 reduce-scatter.8
  1548.8 18.0 reduce-scatter.10
  1569.8 18.0 reduce-scatter.6
where the time goes:
time: 1600 us; the launch traced here: 1590 us
  blocking collectives  708 us (44%)
  other arithmetic  526 us (33%)
  matrix products  203 us (13%)
  waiting for transfers between devices  79.2 us (5%)
  local copies, waits for them, and re-layouts  62.8 us (4%)
    psum x1, blocking collectives, sum_states(): return lax.psum(states, 'atoms').astype(jnp.bfloat16)  355 us
    psum x1, blocking collectives, sum_grads(): return lax.psum(state_grads, 'atoms').astype(jnp.bfloat16)  353 us
    sub x11, other arithmetic, rotate(): leading * cosine - trailing * sine_val  219 us
    another operation x22, other arithmetic  215 us
    dot_general x11, matrix products, query_step(): jnp.einsum('nb,gab->gna', grad_live, state_group, preferred_element_type=...  42.8 us
    dot_general x11, matrix products, key_step(): jnp.einsum('gna,gab->nb', key_rot, grad_group, preferred_element_type=jnp...  41.7 us
    dot_general x11, matrix products, query_step(): jnp.einsum('gna,gab->gnb', query_rot, state_group, preferred_element_type...  37.3 us
    add x11, other arithmetic, query_step(): query_total + jnp.sum(rotate(dir_scale[:, None, None] * back_proj, cosine...  37 us
  transfers between devices with their start and end apart: 4, of which 4 were waited for; matrix products, arithmetic and copies ran while one was open for 0% of the time, Pallas kernels for 0%

commit v1 on v0

v1 whole, which is shorter than its diff:
```python
import functools
import math

import jax
import jax.numpy as jnp
from jax import lax
from jax.experimental import pallas as pl
from jax.experimental.pallas import tpu as pltpu
from jax.sharding import PartitionSpec as P

F32 = jnp.float32
BF16 = jnp.bfloat16

ATOMS = 2048
HALF = ATOMS // 2
FEAT = 128
FREQS = 32
DIRS = 44
GROUP = 4
STEPS = DIRS // GROUP
ROWS = GROUP * FEAT
WIDTH = 256

SINE = (
    4.442882919124345,
    -7.3082456865090855,
    3.606354218433185,
    -0.8461116503751638,
    0.10982451642692614,
)
COSINE = (
    1.4142134962552289,
    -6.978850948563847,
    5.739460376907657,
    -1.8835579059891776,
    0.3106880275307806,
)

CORE_RS, X_RS, Z_RS, Y_RS, Y_AG, Z_AG, X_AG, CORE_AG = 0, 1, 4, 7, 8, 9, 12, 15
MESSAGES = 16
LAGS = (0, 1, 3, 4, 5, 6, 7, 9, 10)


def horner(coefficients, square):
    total = square * coefficients[-1] + coefficients[-2]
    for coefficient in coefficients[-3::-1]:
        total = total * square + coefficient
    return total


def cos_sin_turns(turns):
    nearest = (turns + 12582912.0) - 12582912.0
    rest = turns - nearest
    square = rest * rest
    sine = horner(SINE, square) * rest
    cosine = horner(COSINE, square)
    return 1.0 - sine * sine, sine * cosine


def tile_of(start, size, unit):
    return pl.ds(pl.multiple_of(start, unit), size)


def kernel(
    freq_ref,
    dirs_ref,
    weight_ref,
    mask_ref,
    q_ref,
    k_ref,
    v_ref,
    g_ref,
    pos_ref,
    species_ref,
    domain_ref,
    gain_ref,
    att_out,
    gq_out,
    gk_out,
    gv_out,
    freq_tile,
    pos_tile,
    gain_tile,
    alive_tile,
    key_t,
    query_t,
    value_t,
    grad_t,
    cos_sin,
    key_rot,
    query_rot,
    back_q,
    back_k,
    att_acc,
    gv_acc,
    gq_acc,
    gk_acc,
    part,
    core_in,
    core_sum,
    x_in,
    x_sum,
    z_in,
    z_sum,
    y_in,
    state,
    out_send,
    out_recv,
    send_sem,
    recv_sem,
    out_send_sem,
    out_recv_sem,
):
    atoms_at = lax.axis_index("atoms")
    dirs_at = lax.axis_index("dirs")
    core = lax.rem(atoms_at, 2)
    z_at = lax.rem(lax.div(atoms_at, 2), 4)
    x_at = lax.rem(lax.div(atoms_at, 8), 4)
    y_at = lax.div(atoms_at, 32)

    def device(y, x, z, c):
        return {"atoms": ((y * 4 + x) * 4 + z) * 2 + c}

    other_core = device(y_at, x_at, z_at, 1 - core)
    other_y = device(1 - y_at, x_at, z_at, core)
    x_far = [lax.rem(x_at + d, 4) for d in range(4)]
    z_far = [lax.rem(z_at + d, 4) for d in range(4)]
    x_peers = [device(y_at, x_far[d], z_at, core) for d in range(4)]
    z_peers = [device(y_at, x_at, z_far[d], core) for d in range(4)]
    other_dirs = {"dirs": 1 - dirs_at}

    barrier = pltpu.get_barrier_semaphore()
    partners = [other_core, other_y, other_dirs] + x_peers[1:] + z_peers[1:]
    for partner in partners:
        pl.semaphore_signal(
            barrier, inc=1, device_id=partner, device_id_type=pl.DeviceIdType.MESH
        )

    core_row = core * ROWS
    x_row = core_row + x_at * FEAT
    z_row = x_row + z_at * 32
    y_row = z_row + y_at * 16

    def message(number, g):
        if number == CORE_RS:
            src = part.at[g, tile_of((1 - core) * ROWS, ROWS, ROWS)]
            dst, to = core_in.at[g], other_core
        elif number < Z_RS:
            d = number - X_RS + 1
            src = core_sum.at[g, tile_of(x_far[d] * FEAT, FEAT, FEAT)]
            dst, to = x_in.at[g, 3 - d], x_peers[d]
        elif number < Y_RS:
            d = number - Z_RS + 1
            src = x_sum.at[g, tile_of(z_far[d] * 32, 32, 32)]
            dst, to = z_in.at[g, 3 - d], z_peers[d]
        elif number == Y_RS:
            src = z_sum.at[g, tile_of((1 - y_at) * 16, 16, 16)]
            dst, to = y_in.at[g], other_y
        elif number == Y_AG:
            src = dst = state.at[g, tile_of(y_row, 16, 16)]
            to = other_y
        elif number < X_AG:
            src = dst = state.at[g, tile_of(z_row, 32, 32)]
            to = z_peers[number - Z_AG + 1]
        elif number < CORE_AG:
            src = dst = state.at[g, tile_of(x_row, FEAT, FEAT)]
            to = x_peers[number - X_AG + 1]
        else:
            src = dst = state.at[g, tile_of(core_row, ROWS, ROWS)]
            to = other_core
        return pltpu.make_async_remote_copy(
            src_ref=src,
            dst_ref=dst,
            send_sem=send_sem.at[number, g],
            recv_sem=recv_sem.at[number, g],
            device_id=to,
            device_id_type=pl.DeviceIdType.MESH,
        )

    def send(first, count, g):
        for number in range(first, first + count):
            message(number, g).start()

    def receive(first, count, g):
        for number in range(first, first + count):
            message(number, g).wait()

    def stage_0(g):
        send(CORE_RS, 1, g)

    def stage_1(g):
        receive(CORE_RS, 1, g)
        mine = part[g, tile_of(core_row, ROWS, ROWS), :].astype(F32)
        core_sum[g] = (mine + core_in[g].astype(F32)).astype(BF16)
        send(X_RS, 3, g)

    def stage_2(g):
        receive(X_RS, 3, g)
        total = core_sum[g, tile_of(x_at * FEAT, FEAT, FEAT), :].astype(F32)
        for slot in range(3):
            total = total + x_in[g, slot].astype(F32)
        x_sum[g] = total
        send(Z_RS, 3, g)

    def stage_3(g):
        receive(Z_RS, 3, g)
        total = x_sum[g, tile_of(z_at * 32, 32, 32), :]
        for slot in range(3):
            total = total + z_in[g, slot]
        z_sum[g] = total
        send(Y_RS, 1, g)

    def stage_4(g):
        receive(Y_RS, 1, g)
        total = z_sum[g, tile_of(y_at * 16, 16, 16), :] + y_in[g]
        state[g, tile_of(y_row, 16, 16), :] = total.astype(BF16)
        send(Y_AG, 1, g)

    def stage_5(g):
        receive(Y_AG, 1, g)
        send(Z_AG, 3, g)

    def stage_6(g):
        receive(Z_AG, 3, g)
        send(X_AG, 3, g)

    def stage_7(g):
        receive(X_AG, 3, g)
        send(CORE_AG, 1, g)

    def stage_8(g):
        receive(CORE_AG, 1, g)

    stages = (stage_0, stage_1, stage_2, stage_3, stage_4, stage_5, stage_6, stage_7, stage_8)

    def exchange(t, lowest, highest):
        for number in range(len(stages) - 1, -1, -1):
            lag = LAGS[number]
            if highest < lag or lowest - lag >= STEPS:
                continue
            if lowest >= lag and highest - lag < STEPS:
                stages[number](t - lag)
            else:

                @pl.when(jnp.logical_and(t >= lag, t < lag + STEPS))
                def _(number=number, lag=lag):
                    stages[number](t - lag)

    for f in range(FREQS):
        freq_tile[f : f + 1, :] = jnp.full((1, 128), freq_ref[f] * (0.5 / math.pi), F32)
    for axis in range(3):
        pos_tile[axis] = jnp.broadcast_to(pos_ref[axis : axis + 1, :], (8, ATOMS))
    for s in range(gain_ref.shape[0]):
        gain_tile[s] = jnp.broadcast_to(gain_ref[s : s + 1, :], (FEAT, FEAT)).T
    alive_tile[...] = jnp.broadcast_to(
        jnp.where(domain_ref[...] == atoms_at, 1.0, 0.0), (8, ATOMS)
    )

    def alive_of(columns):
        return jnp.concatenate([alive_tile[:, columns]] * (FEAT // 8), axis=0)

    def gain_of(columns):
        species = jnp.broadcast_to(species_ref[:, columns], (FEAT, 128))
        gain = gain_tile[0]
        for s in range(1, gain_ref.shape[0]):
            gain = jnp.where(species == s, gain_tile[s], gain)
        return gain * alive_of(columns)

    def prepare(block, carry):
        columns = tile_of(block * 128, 128, 128)
        key_t[:, columns] = (k_ref[columns, :].astype(F32).T * gain_of(columns)).astype(BF16)
        query_t[:, columns] = (q_ref[columns, :].astype(F32).T * alive_of(columns)).astype(BF16)
        value_t[:, columns] = v_ref[columns, :].astype(F32).T.astype(BF16)
        grad_t[:, columns] = g_ref[columns, :].astype(F32).T.astype(BF16)
        return carry

    lax.fori_loop(0, ATOMS // 128, prepare, 0)

    def coef(u):
        return weight_ref[u] * mask_ref[u].astype(F32) * (1.0 / math.sqrt(FEAT * ATOMS))

    def rotate_to(x_ref, y_ref, u, p, columns, place, cosine, sine):
        lead = x_ref[p : p + 16, columns]
        trail = x_ref[p + 64 : p + 80, columns]
        y_ref[u, p : p + 16, place] = lead * cosine - trail * sine
        y_ref[u, p + 64 : p + 80, place] = lead * sine + trail * cosine

    def state_step(i):
        for u in range(GROUP):
            at = i * GROUP + u
            for low in range(0, ATOMS, WIDTH):
                columns = pl.ds(low, WIDTH)
                projected = (
                    dirs_ref[0, at] * pos_tile[0, :, columns]
                    + dirs_ref[1, at] * pos_tile[1, :, columns]
                    + dirs_ref[2, at] * pos_tile[2, :, columns]
                )
                for low_f in range(0, FREQS, 16):
                    pairs = []
                    for f in (low_f, low_f + 8):
                        freq = jnp.concatenate([freq_tile[f : f + 8, :]] * (WIDTH // 128), axis=1)
                        pairs.append(cos_sin_turns(projected * freq))
                    cosine = jnp.concatenate([pairs[0][0], pairs[1][0]], axis=0).astype(BF16)
                    sine = jnp.concatenate([pairs[0][1], pairs[1][1]], axis=0).astype(BF16)
                    cos_sin[at, 0, low_f : low_f + 16, columns] = cosine
                    cos_sin[at, 1, low_f : low_f + 16, columns] = sine
                    for p in (low_f, low_f + FREQS):
                        rotate_to(key_t, key_rot, u, p, columns, columns, cosine, sine)
                        rotate_to(query_t, query_rot, u, p, columns, columns, cosine, sine)
        for at_row, rotated, rows in ((0, key_rot, v_ref), (ROWS, query_rot, g_ref)):
            product = jnp.dot(
                rotated[...].reshape(ROWS, ATOMS), rows[...], preferred_element_type=F32
            )
            for u in range(GROUP):
                part[i, at_row + u * FEAT : at_row + (u + 1) * FEAT, :] = (
                    product[u * FEAT : (u + 1) * FEAT] * coef(i * GROUP + u)
                ).astype(BF16)

    def output_step(i, base):
        for u in range(GROUP):
            at = i * GROUP + u
            for low in range(0, HALF, WIDTH):
                place = pl.ds(low, WIDTH)
                columns = tile_of(base + low, WIDTH, WIDTH)
                for low_f in range(0, FREQS, 16):
                    cosine = cos_sin[at, 0, low_f : low_f + 16, columns]
                    sine = cos_sin[at, 1, low_f : low_f + 16, columns]
                    for p in (low_f, low_f + FREQS):
                        rotate_to(key_t, key_rot, u, p, columns, place, cosine, sine)
                        rotate_to(query_t, query_rot, u, p, columns, place, cosine, sine)
        columns = tile_of(base, HALF, HALF)
        forward = state[i, :ROWS, :]
        backward = state[i, ROWS:, :]
        contract = (((0,), (0,)), ((), ()))
        for matrix, rotated, rows_t, total, back in (
            (forward, query_rot, grad_t, att_acc, back_q),
            (backward, key_rot, value_t, gv_acc, back_k),
        ):
            back[...] = (
                jnp.dot(matrix, rows_t[:, columns], preferred_element_type=F32)
                .astype(BF16)
                .reshape(GROUP, FEAT, HALF)
            )
            total[...] += lax.dot_general(
                matrix,
                rotated[:, :, :HALF].reshape(ROWS, HALF),
                contract,
                preferred_element_type=F32,
            )
        for low in range(0, HALF, WIDTH):
            place = pl.ds(low, WIDTH)
            columns = tile_of(base + low, WIDTH, WIDTH)
            for low_f in range(0, FREQS, 16):
                cosines = [
                    cos_sin[i * GROUP + u, 0, low_f : low_f + 16, columns] for u in range(GROUP)
                ]
                sines = [
                    cos_sin[i * GROUP + u, 1, low_f : low_f + 16, columns] for u in range(GROUP)
                ]
                for p in (low_f, low_f + FREQS):
                    for back, total in ((back_q, gq_acc), (back_k, gk_acc)):
                        lead_sum = trail_sum = None
                        for u in range(GROUP):
                            lead = back[u, p : p + 16, place]
                            trail = back[u, p + 64 : p + 80, place]
                            new_lead = lead * cosines[u] + trail * sines[u]
                            new_trail = trail * cosines[u] - lead * sines[u]
                            lead_sum = new_lead if u == 0 else lead_sum + new_lead
                            trail_sum = new_trail if u == 0 else trail_sum + new_trail
                        total[p : p + 16, place] += lead_sum.astype(F32)
                        total[p + 64 : p + 80, place] += trail_sum.astype(F32)

    totals = (att_acc, gq_acc, gk_acc, gv_acc)

    def clear():
        for total in totals:
            total[...] = jnp.zeros_like(total)

    pl.semaphore_wait(barrier, len(partners))

    def first_loop(t, carry):
        state_step(t)
        exchange(t, 0, STEPS - 1)
        return carry

    lax.fori_loop(0, STEPS, first_loop, 0)

    clear()
    far_base = (1 - dirs_at) * HALF

    def second_loop(i, carry):
        exchange(i + STEPS, STEPS, 2 * STEPS - 1)
        output_step(i, far_base)
        return carry

    lax.fori_loop(0, STEPS, second_loop, 0)

    def out_message(n):
        return pltpu.make_async_remote_copy(
            src_ref=out_send.at[n],
            dst_ref=out_recv.at[n],
            send_sem=out_send_sem.at[n],
            recv_sem=out_recv_sem.at[n],
            device_id=other_dirs,
            device_id_type=pl.DeviceIdType.MESH,
        )

    for n, total in enumerate(totals):
        out_send[n] = total[...].astype(BF16)
        out_message(n).start()
    clear()
    near_base = dirs_at * HALF

    def third_loop(i, carry):
        output_step(i, near_base)
        return carry

    lax.fori_loop(0, STEPS, third_loop, 0)

    for n in range(4):
        out_message(n).wait()

    def finish(block, carry):
        place = tile_of(block * 128, 128, 128)
        columns = tile_of(near_base + block * 128, 128, 128)
        alive = alive_of(columns)
        for n, (total, out, factor) in enumerate(
            zip(
                totals,
                (att_out, gq_out, gk_out, gv_out),
                (None, alive, gain_of(columns), None),
            )
        ):
            whole = total[:, place] + out_recv[n, :, place].astype(F32)
            if factor is not None:
                whole = whole * factor
            out[place, :] = whole.T.astype(BF16)
        return carry

    lax.fori_loop(0, HALF // 128, finish, 0)


def per_device(
    queries,
    keys,
    values,
    cotangent,
    positions,
    species,
    domain,
    species_gain,
    frequency,
    directions,
    dir_weight,
    dir_mask,
):
    smem = pl.BlockSpec(memory_space=pltpu.SMEM)
    vmem = pl.BlockSpec(memory_space=pltpu.VMEM)
    species_count = species_gain.shape[0]
    scratch = [
        pltpu.VMEM((FREQS, 128), F32),
        pltpu.VMEM((3, 8, ATOMS), F32),
        pltpu.VMEM((species_count, FEAT, FEAT), F32),
        pltpu.VMEM((8, ATOMS), F32),
        pltpu.VMEM((FEAT, ATOMS), BF16),
        pltpu.VMEM((FEAT, ATOMS), BF16),
        pltpu.VMEM((FEAT, ATOMS), BF16),
        pltpu.VMEM((FEAT, ATOMS), BF16),
        pltpu.VMEM((DIRS, 2, FREQS, ATOMS), BF16),
        pltpu.VMEM((GROUP, FEAT, ATOMS), BF16),
        pltpu.VMEM((GROUP, FEAT, ATOMS), BF16),
        pltpu.VMEM((GROUP, FEAT, HALF), BF16),
        pltpu.VMEM((GROUP, FEAT, HALF), BF16),
        pltpu.VMEM((FEAT, HALF), F32),
        pltpu.VMEM((FEAT, HALF), F32),
        pltpu.VMEM((FEAT, HALF), F32),
        pltpu.VMEM((FEAT, HALF), F32),
        pltpu.VMEM((STEPS, 2 * ROWS, FEAT), BF16),
        pltpu.VMEM((STEPS, ROWS, FEAT), BF16),
        pltpu.VMEM((STEPS, ROWS, FEAT), BF16),
        pltpu.VMEM((STEPS, 3, FEAT, FEAT), BF16),
        pltpu.VMEM((STEPS, FEAT, FEAT), F32),
        pltpu.VMEM((STEPS, 3, 32, FEAT), F32),
        pltpu.VMEM((STEPS, 32, FEAT), F32),
        pltpu.VMEM((STEPS, 16, FEAT), F32),
        pltpu.VMEM((STEPS, 2 * ROWS, FEAT), BF16),
        pltpu.VMEM((4, FEAT, HALF), BF16),
        pltpu.VMEM((4, FEAT, HALF), BF16),
        pltpu.SemaphoreType.DMA((MESSAGES, STEPS)),
        pltpu.SemaphoreType.DMA((MESSAGES, STEPS)),
        pltpu.SemaphoreType.DMA((4,)),
        pltpu.SemaphoreType.DMA((4,)),
    ]
    att, gq, gk, gv = pl.pallas_call(
        kernel,
        out_shape=[jax.ShapeDtypeStruct((HALF, FEAT), BF16)] * 4,
        in_specs=[smem] * 4 + [vmem] * 8,
        out_specs=[vmem] * 4,
        scratch_shapes=scratch,
        compiler_params=pltpu.CompilerParams(
            collective_id=0, has_side_effects=True, vmem_limit_bytes=56 * 2**20
        ),
        name="fast_attention",
    )(
        frequency,
        directions,
        dir_weight,
        dir_mask,
        queries,
        keys,
        values,
        cotangent,
        positions,
        species.reshape(1, ATOMS),
        domain.reshape(1, ATOMS),
        species_gain,
    )
    return att, gq, gk, gv


def solution(mesh):
    return jax.shard_map(
        per_device,
        mesh=mesh,
        in_specs=(
            P("atoms", None),
            P("atoms", None),
            P("atoms", None),
            P("atoms", None),
            P(None, "atoms"),
            P("atoms"),
            P("atoms"),
            P(),
            P(),
            P(None, "dirs"),
            P("dirs"),
            P("dirs"),
        ),
        out_specs=(
            P(("atoms", "dirs"), None),
            P(("atoms", "dirs"), None),
            P(("atoms", "dirs"), None),
            P(("atoms", "dirs"), None),
        ),
        check_vma=False,
    )
```

time: 1600 us -> 111 us (0.07)
  blocking collectives: 708 us -> 0 us
  other arithmetic: 526 us -> 0 us
  matrix products: 203 us -> 0 us
  Pallas kernels: 0 us -> 106 us
  waiting for transfers between devices: 79.2 us -> 0 us
  local copies, waits for them, and re-layouts: 62.8 us -> 4.5 us
    psum x2 -> x0, blocking collectives: 708 us -> none  [the longest x1 355 us: sum_states(): return lax.psum(states, 'atoms').astype(jnp.bfloat16)]
    sub x11 -> x0, other arithmetic: 219 us -> none  [rotate(): leading * cosine - trailing * sine_val]
    another operation x22 -> x0, other arithmetic: 215 us -> none
    dot_general x66 -> x0, matrix products: 203 us -> none  [the longest x11 42.8 us: query_step(): jnp.einsum('nb,gab->gna', grad_live, state_group, preferred_element_type=...]
    pallas_call x0 -> x1, Pallas kernels: none -> 106 us  [per_device(): pl.pallas_call(kernel, out_shape=[jax.ShapeDtypeStruct((HALF, FEAT), BF16...]
    reduce_scatter x4 -> x0, waiting for transfers between devices: 78.5 us -> none  [the longest x1 21.1 us: per_device(): lax.psum_scatter(key_terms.astype(jnp.bfloat16), 'dirs', scatter_dimensio...]
    add x23 -> x0, other arithmetic: 63.2 us -> none  [the longest x11 37 us: query_step(): query_total + jnp.sum(rotate(dir_scale[:, None, None] * back_proj, cosine...]
    slice x35 -> x0, local copies, waits for them, and re-layouts: 29.6 us -> none  [the longest x33 27.3 us: rotate(): leading = features[..., :half_width]]
  transfers between devices with their start and end apart: 4 -> 0, of which waited for: 4 -> 0; matrix products, arithmetic and copies ran while one was open for 0% -> 0% of each run, Pallas kernels for 0% -> 0%
where the time goes in v1:
time: 111 us
  Pallas kernels  106 us (95%)
  local copies, waits for them, and re-layouts  4.5 us (4%)
    pallas_call x1, Pallas kernels, per_device(): pl.pallas_call(kernel, out_shape=[jax.ShapeDtypeStruct((HALF, FEAT), BF16...  106 us
    unnamed x10, local copies, waits for them, and re-layouts  4.5 us

profile of v1, /device:TPU:1, one launch (start us, length us, event | category | flops | bytes accessed | tf_op | source)
XLA Modules:
  0.0 111.2 jit_solution(13459189724373605108)
XLA Ops:
  0.6 106.0 %fast_attention.1 = (bf16[1024,128]{1,0:T(8,128)(2,1)}, bf16[1024,128]{1,0:T(8,128)(2,1)}, bf16[1024,128]{1,0:T(8,128)(2,1)}, bf16[1024,128]{1,0:T(8,128)(2,1)}) custom-call(f32[32]{0:T(128)} %freq_ref.1, f32[3,44]{1,0:T(4,128)} %dirs_ref.1, f32[44]{0:T(128)} %weight_ref.1, s32[44]{0:T(128)} %mask_ref.1, bf16[2048,128]{1,0:T(8,128)(2,1)} %q_ref.1, ...), custom_call_target="tpu_custom_call" | custom-call | tf_op jit(solution)/shard_map/fast_attention/pallas_call | solution.py:494
  106.7 0.0 copy-start.2
  106.7 1.7 %copy.20 = bf16[1024,128]{1,0:T(8,128)(2,1)} copy(bf16[1024,128]{1,0:T(8,128)(2,1)} %get-tuple-element.8) | data formatting | bytes 524288
  108.4 0.0 copy-done.2
  108.4 0.0 copy-start.1
  108.4 0.7 copy.21
  109.1 0.3 copy-done.1
  109.4 0.0 copy-start
  109.4 0.7 copy.22
  110.1 0.3 copy-done
  110.5 0.7 copy.23
Async XLA Ops:
  106.7 1.7 %copy-start.2 = (bf16[1024,128]{1,0:T(8,128)(2,1)S(1)}, bf16[1024,128]{1,0:T(8,128)(2,1)}, u32[]{:S(2)}) copy-start(bf16[1024,128]{1,0:T(8,128)(2,1)} %get-tuple-element.9) | copy-start | bytes 786436
  108.4 1.0 copy-start.1
  109.4 1.0 copy-start

commit v2 on v1

v2 whole, which is shorter than its diff:
```python
import functools
import math

import jax
import jax.numpy as jnp
from jax import lax
from jax.experimental import pallas as pl
from jax.experimental.pallas import tpu as pltpu
from jax.sharding import PartitionSpec as P

F32 = jnp.float32
BF16 = jnp.bfloat16

ATOMS = 2048
HALF = ATOMS // 2
FEAT = 128
FREQS = 32
DIRS = 44
GROUP = 4
STEPS = DIRS // GROUP
ROWS = GROUP * FEAT
WIDTH = 256

SINE = (
    4.442882919124345,
    -7.3082456865090855,
    3.606354218433185,
    -0.8461116503751638,
    0.10982451642692614,
)
COSINE = (
    1.4142134962552289,
    -6.978850948563847,
    5.739460376907657,
    -1.8835579059891776,
    0.3106880275307806,
)

CORE_RS, RING_RS, HOP_RS, LINE_RS, Y_RS = 0, 1, 3, 5, 8
Y_AG, LINE_AG, RING_AG, HOP_AG, CORE_AG = 9, 12, 15, 17, 19
MESSAGES = 20
STAGES = 11


def horner(coefficients, square):
    total = square * coefficients[-1] + coefficients[-2]
    for coefficient in coefficients[-3::-1]:
        total = total * square + coefficient
    return total


def cos_sin_turns(turns):
    nearest = (turns + 12582912.0) - 12582912.0
    rest = turns - nearest
    square = rest * rest
    sine = horner(SINE, square) * rest
    cosine = horner(COSINE, square)
    return 1.0 - sine * sine, sine * cosine


def tile_of(start, size, unit):
    return pl.ds(pl.multiple_of(start, unit), size)


def kernel(
    freq_ref,
    dirs_ref,
    weight_ref,
    mask_ref,
    dirs_rows_ref,
    q_ref,
    k_ref,
    v_ref,
    g_ref,
    pos_ref,
    species_ref,
    domain_ref,
    gain_ref,
    att_out,
    gq_out,
    gk_out,
    gv_out,
    freq_tile,
    pos_tile,
    gain_tile,
    alive_tile,
    key_t,
    query_t,
    value_t,
    grad_t,
    cos_sin,
    far_cos_sin,
    key_rot,
    query_rot,
    back_q,
    back_k,
    att_acc,
    gv_acc,
    gq_acc,
    gk_acc,
    part,
    core_in,
    core_sum,
    ring_in,
    relay,
    hop_in,
    line_sum,
    line_in,
    y_sum,
    y_in,
    state,
    dirs_send,
    dirs_recv,
    far_dirs,
    send_sem,
    recv_sem,
    dirs_sem,
):
    atoms_at = lax.axis_index("atoms")
    dirs_at = lax.axis_index("dirs")
    core = lax.rem(atoms_at, 2)
    z_at = lax.rem(lax.div(atoms_at, 2), 4)
    x_at = lax.rem(lax.div(atoms_at, 8), 4)
    y_at = lax.div(atoms_at, 32)
    near_base = dirs_at * HALF
    far_base = HALF - near_base

    def along(at, step, stride):
        return atoms_at + (lax.rem(at + step, 4) - at) * stride

    other_core = {"atoms": atoms_at + 1 - 2 * core}
    y_far = atoms_at + 32 - 64 * y_at
    y_peers = [
        {"atoms": y_far, "dirs": dirs_at},
        {"atoms": atoms_at, "dirs": 1 - dirs_at},
        {"atoms": y_far, "dirs": 1 - dirs_at},
    ]

    barrier = pltpu.get_barrier_semaphore()
    partners = [other_core] + y_peers
    for step in range(1, 4):
        partners += [{"atoms": along(x_at, step, 8)}, {"atoms": along(z_at, step, 2)}]
    for partner in partners:
        pl.semaphore_signal(
            barrier, inc=1, device_id=partner, device_id_type=pl.DeviceIdType.MESH
        )

    core_row = core * ROWS

    def place_of(g):
        odd = lax.rem(g, 2)
        first = x_at + odd * (z_at - x_at)
        second = z_at + odd * (x_at - z_at)
        return first, second, 8 - 6 * odd, 2 + 6 * odd

    def rows_of(g, step):
        first, _, _, _ = place_of(g)
        return core_row + lax.rem(first + step, 4) * FEAT

    def message(number, g):
        first, second, first_stride, second_stride = place_of(g)
        ahead = {"atoms": along(first, 1, first_stride)}
        behind = {"atoms": along(first, 3, first_stride)}
        first_row = core_row + first * FEAT
        second_row = first_row + second * 32
        y_row = second_row + y_at * 16
        if number == CORE_RS:
            src = part.at[g, tile_of((1 - core) * ROWS, ROWS, ROWS)]
            dst, to = core_in.at[g], other_core
        elif number < HOP_RS:
            side = number - RING_RS
            src = core_sum.at[g, tile_of(lax.rem(first + 2, 4) * FEAT + 64 * side, 64, 64)]
            dst, to = ring_in.at[g, side], (ahead, behind)[side]
        elif number < LINE_RS:
            side = number - HOP_RS
            src, dst, to = relay.at[g, side], hop_in.at[g, side], (ahead, behind)[side]
        elif number < Y_RS:
            step = number - LINE_RS + 1
            src = line_sum.at[g, tile_of(lax.rem(second + step, 4) * 32, 32, 32)]
            dst, to = line_in.at[g, 3 - step], {"atoms": along(second, step, second_stride)}
        elif number == Y_RS:
            src = y_sum.at[g, tile_of((1 - y_at) * 16, 16, 16)]
            dst, to = y_in.at[g], y_peers[0]
        elif number < LINE_AG:
            src = dst = state.at[dirs_at, g, tile_of(y_row, 16, 16)]
            to = y_peers[number - Y_AG]
        elif number < RING_AG:
            src = dst = state.at[:, g, tile_of(second_row, 32, 32)]
            to = {"atoms": along(second, number - LINE_AG + 1, second_stride)}
        elif number < HOP_AG:
            src = dst = state.at[:, g, tile_of(first_row, FEAT, FEAT)]
            to = (ahead, behind)[number - RING_AG]
        elif number < CORE_AG:
            side = number - HOP_AG
            src = dst = state.at[:, g, tile_of(rows_of(g, (3, 1)[side]) + 64 * side, 64, 64)]
            to = (ahead, behind)[side]
        else:
            src = dst = state.at[:, g, tile_of(core_row, ROWS, ROWS)]
            to = other_core
        return pltpu.make_async_remote_copy(
            src_ref=src,
            dst_ref=dst,
            send_sem=send_sem.at[number, g],
            recv_sem=recv_sem.at[number, g],
            device_id=to,
            device_id_type=pl.DeviceIdType.MESH,
        )

    first_of = (
        CORE_RS, RING_RS, HOP_RS, LINE_RS, Y_RS, Y_AG, LINE_AG, RING_AG, HOP_AG, CORE_AG, MESSAGES
    )

    def stage(number, g):
        if number > 0:
            for n in range(first_of[number - 1], first_of[number]):
                message(n, g).wait()
        if number == 1:
            mine = part[g, tile_of(core_row, ROWS, ROWS), :].astype(F32)
            core_sum[g] = (mine + core_in[g].astype(F32)).astype(BF16)
        elif number == 2:
            for side, step in ((0, 1), (1, 3)):
                rows = lax.rem(place_of(g)[0] + step, 4) * FEAT
                met, kept = rows + 64 * side, rows + 64 * (1 - side)
                total = core_sum[g, tile_of(met, 64, 64), :].astype(F32)
                total = total + ring_in[g, side].astype(F32)
                relay[g, side, 64 * side : 64 * side + 64, :] = total.astype(BF16)
                relay[g, side, 64 * (1 - side) : 64 * (1 - side) + 64, :] = core_sum[
                    g, tile_of(kept, 64, 64), :
                ]
        elif number == 3:
            total = core_sum[g, tile_of(place_of(g)[0] * FEAT, FEAT, FEAT), :].astype(F32)
            total = total + hop_in[g, 0].astype(F32) + hop_in[g, 1].astype(F32)
            line_sum[g] = total.astype(BF16)
        elif number == 4:
            total = line_sum[g, tile_of(place_of(g)[1] * 32, 32, 32), :].astype(F32)
            for slot in range(3):
                total = total + line_in[g, slot].astype(F32)
            y_sum[g] = total
        elif number == 5:
            first, second, _, _ = place_of(g)
            row = core_row + first * FEAT + second * 32 + y_at * 16
            total = y_sum[g, tile_of(y_at * 16, 16, 16), :] + y_in[g]
            state[dirs_at, g, tile_of(row, 16, 16), :] = total.astype(BF16)
        if number < STAGES - 1:
            for n in range(first_of[number], first_of[number + 1]):
                message(n, g).start()

    def exchange(t, lowest, highest):
        for number in range(STAGES - 1, -1, -1):
            if highest < number or lowest - number >= STEPS:
                continue
            if lowest >= number and highest - number < STEPS:
                stage(number, t - number)
            else:

                @pl.when(jnp.logical_and(t >= number, t < number + STEPS))
                def _(number=number):
                    stage(number, t - number)

    dirs_send[...] = jnp.zeros_like(dirs_send)
    dirs_send[0:3, 0:DIRS] = dirs_rows_ref[...]
    for f in range(FREQS):
        freq_tile[f : f + 1, :] = jnp.full((1, 128), freq_ref[f] * (0.5 / math.pi), F32)
    for base, low in ((near_base, 0), (far_base, HALF)):
        columns = tile_of(base, HALF, HALF)
        for axis in range(3):
            pos_tile[axis, :, low : low + HALF] = jnp.broadcast_to(
                pos_ref[axis : axis + 1, columns], (8, HALF)
            )
        alive_tile[:, low : low + HALF] = jnp.broadcast_to(
            jnp.where(domain_ref[:, columns] == atoms_at, 1.0, 0.0), (8, HALF)
        )
    for s in range(gain_ref.shape[0]):
        gain_tile[s] = jnp.broadcast_to(gain_ref[s : s + 1, :], (FEAT, FEAT)).T

    def alive_of(place):
        return jnp.concatenate([alive_tile[:, place]] * (FEAT // 8), axis=0)

    def gain_of(place, columns):
        species = jnp.broadcast_to(species_ref[:, columns], (FEAT, 128))
        gain = gain_tile[0]
        for s in range(1, gain_ref.shape[0]):
            gain = jnp.where(species == s, gain_tile[s], gain)
        return gain * alive_of(place)

    def prepare(block, carry):
        for base, low in ((near_base, 0), (far_base, HALF)):
            columns = tile_of(base + block * 128, 128, 128)
            place = tile_of(low + block * 128, 128, 128)
            keys = k_ref[columns, :].astype(F32).T * gain_of(place, columns)
            key_t[:, place] = keys.astype(BF16)
            query_t[:, place] = (q_ref[columns, :].astype(F32).T * alive_of(place)).astype(BF16)
            if low == 0:
                value_t[:, place] = v_ref[columns, :].astype(F32).T.astype(BF16)
                grad_t[:, place] = g_ref[columns, :].astype(F32).T.astype(BF16)
        return carry

    lax.fori_loop(0, HALF // 128, prepare, 0)

    def coef(u):
        return weight_ref[u] * mask_ref[u].astype(F32) * (1.0 / math.sqrt(FEAT * ATOMS))

    def rotate_to(x_ref, y_ref, u, p, columns, cosine, sine):
        lead = x_ref[p : p + 16, columns]
        trail = x_ref[p + 64 : p + 80, columns]
        y_ref[u, p : p + 16, columns] = lead * cosine - trail * sine
        y_ref[u, p + 64 : p + 80, columns] = lead * sine + trail * cosine

    def angles(dirs, at, columns):
        projected = (
            dirs[0, at] * pos_tile[0, :, columns]
            + dirs[1, at] * pos_tile[1, :, columns]
            + dirs[2, at] * pos_tile[2, :, columns]
        )
        for low_f in range(0, FREQS, 16):
            pairs = []
            for f in (low_f, low_f + 8):
                freq = jnp.concatenate([freq_tile[f : f + 8, :]] * (WIDTH // 128), axis=1)
                pairs.append(cos_sin_turns(projected * freq))
            cosine = jnp.concatenate([pairs[0][0], pairs[1][0]], axis=0).astype(BF16)
            sine = jnp.concatenate([pairs[0][1], pairs[1][1]], axis=0).astype(BF16)
            yield low_f, cosine, sine

    def state_step(i):
        for u in range(GROUP):
            at = i * GROUP + u
            for low in range(0, ATOMS, WIDTH):
                columns = pl.ds(low, WIDTH)
                for low_f, cosine, sine in angles(dirs_ref, at, columns):
                    if low < HALF:
                        cos_sin[at, 0, low_f : low_f + 16, columns] = cosine
                        cos_sin[at, 1, low_f : low_f + 16, columns] = sine
                    for p in (low_f, low_f + FREQS):
                        rotate_to(key_t, key_rot, u, p, columns, cosine, sine)
                        rotate_to(query_t, query_rot, u, p, columns, cosine, sine)
        for at_row, rotated, rows in ((0, key_rot, v_ref), (ROWS, query_rot, g_ref)):
            product = jnp.zeros((ROWS, FEAT), F32)
            for base, low in ((near_base, 0), (far_base, HALF)):
                product = product + jnp.dot(
                    rotated[:, :, low : low + HALF].reshape(ROWS, HALF),
                    rows[tile_of(base, HALF, HALF), :],
                    preferred_element_type=F32,
                )
            for u in range(GROUP):
                part[i, at_row + u * FEAT : at_row + (u + 1) * FEAT, :] = (
                    product[u * FEAT : (u + 1) * FEAT] * coef(i * GROUP + u)
                ).astype(BF16)

    def output_step(i, far):
        low_at = far * HALF
        for u in range(GROUP):
            at = i * GROUP + u
            for low in range(0, HALF, WIDTH):
                columns = pl.ds(low, WIDTH)
                if far:
                    table = angles(far_dirs, at, columns)
                else:
                    table = (
                        (
                            low_f,
                            cos_sin[at, 0, low_f : low_f + 16, columns],
                            cos_sin[at, 1, low_f : low_f + 16, columns],
                        )
                        for low_f in range(0, FREQS, 16)
                    )
                for low_f, cosine, sine in table:
                    if far:
                        far_cos_sin[u, 0, low_f : low_f + 16, columns] = cosine
                        far_cos_sin[u, 1, low_f : low_f + 16, columns] = sine
                    for p in (low_f, low_f + FREQS):
                        for x_ref, y_ref in ((key_t, key_rot), (query_t, query_rot)):
                            lead = x_ref[p : p + 16, columns]
                            trail = x_ref[p + 64 : p + 80, columns]
                            place = pl.ds(low_at + low, WIDTH)
                            y_ref[u, p : p + 16, place] = lead * cosine - trail * sine
                            y_ref[u, p + 64 : p + 80, place] = lead * sine + trail * cosine
        owner = 1 - dirs_at if far else dirs_at
        forward = state[owner, i, :ROWS, :]
        backward = state[owner, i, ROWS:, :]
        contract = (((0,), (0,)), ((), ()))
        for matrix, rotated, rows_t, total, back in (
            (forward, query_rot, grad_t, att_acc, back_q),
            (backward, key_rot, value_t, gv_acc, back_k),
        ):
            back[far] = (
                jnp.dot(matrix, rows_t[...], preferred_element_type=F32)
                .astype(BF16)
                .reshape(GROUP, FEAT, HALF)
            )
            total[...] += lax.dot_general(
                matrix,
                rotated[:, :, low_at : low_at + HALF].reshape(ROWS, HALF),
                contract,
                preferred_element_type=F32,
            )
        for low in range(0, HALF, WIDTH):
            columns = pl.ds(low, WIDTH)
            for low_f in range(0, FREQS, 16):
                if far:
                    tables = [far_cos_sin[u, :, low_f : low_f + 16, columns] for u in range(GROUP)]
                else:
                    tables = [
                        cos_sin[i * GROUP + u, :, low_f : low_f + 16, columns] for u in range(GROUP)
                    ]
                for p in (low_f, low_f + FREQS):
                    for back, total in ((back_q, gq_acc), (back_k, gk_acc)):
                        lead_sum = trail_sum = None
                        for u in range(GROUP):
                            cosine, sine = tables[u][0], tables[u][1]
                            lead = back[far, u, p : p + 16, columns]
                            trail = back[far, u, p + 64 : p + 80, columns]
                            new_lead = lead * cosine + trail * sine
                            new_trail = trail * cosine - lead * sine
                            lead_sum = new_lead if u == 0 else lead_sum + new_lead
                            trail_sum = new_trail if u == 0 else trail_sum + new_trail
                        total[p : p + 16, columns] += lead_sum.astype(F32)
                        total[p + 64 : p + 80, columns] += trail_sum.astype(F32)

    totals = (att_acc, gq_acc, gk_acc, gv_acc)
    for total in totals:
        total[...] = jnp.zeros_like(total)

    pl.semaphore_wait(barrier, len(partners))

    dirs_copy = pltpu.make_async_remote_copy(
        src_ref=dirs_send,
        dst_ref=dirs_recv,
        send_sem=dirs_sem.at[0],
        recv_sem=dirs_sem.at[1],
        device_id=y_peers[1],
        device_id_type=pl.DeviceIdType.MESH,
    )
    dirs_copy.start()

    def first_loop(t, carry):
        state_step(t)
        exchange(t, 0, STEPS - 1)
        return carry

    lax.fori_loop(0, STEPS, first_loop, 0)

    dirs_copy.wait()
    to_scalars = pltpu.make_async_copy(dirs_recv, far_dirs, dirs_sem.at[2])
    to_scalars.start()
    to_scalars.wait()

    def second_loop(i, carry):
        exchange(i + STEPS, STEPS, 2 * STEPS - 1)
        output_step(i, 0)
        output_step(i, 1)
        return carry

    lax.fori_loop(0, STEPS, second_loop, 0)

    def finish(block, carry):
        place = tile_of(block * 128, 128, 128)
        alive = alive_of(place)
        gain = gain_of(place, tile_of(near_base + block * 128, 128, 128))
        for total, out, factor in zip(
            totals, (att_out, gq_out, gk_out, gv_out), (None, alive, gain, None)
        ):
            whole = total[:, place]
            if factor is not None:
                whole = whole * factor
            out[place, :] = whole.T.astype(BF16)
        return carry

    lax.fori_loop(0, HALF // 128, finish, 0)


def per_device(
    queries,
    keys,
    values,
    cotangent,
    positions,
    species,
    domain,
    species_gain,
    frequency,
    directions,
    dir_weight,
    dir_mask,
):
    smem = pl.BlockSpec(memory_space=pltpu.SMEM)
    vmem = pl.BlockSpec(memory_space=pltpu.VMEM)
    species_count = species_gain.shape[0]
    scratch = [
        pltpu.VMEM((FREQS, 128), F32),
        pltpu.VMEM((3, 8, ATOMS), F32),
        pltpu.VMEM((species_count, FEAT, FEAT), F32),
        pltpu.VMEM((8, ATOMS), F32),
        pltpu.VMEM((FEAT, ATOMS), BF16),
        pltpu.VMEM((FEAT, ATOMS), BF16),
        pltpu.VMEM((FEAT, HALF), BF16),
        pltpu.VMEM((FEAT, HALF), BF16),
        pltpu.VMEM((DIRS, 2, FREQS, HALF), BF16),
        pltpu.VMEM((GROUP, 2, FREQS, HALF), BF16),
        pltpu.VMEM((GROUP, FEAT, ATOMS), BF16),
        pltpu.VMEM((GROUP, FEAT, ATOMS), BF16),
        pltpu.VMEM((2, GROUP, FEAT, HALF), BF16),
        pltpu.VMEM((2, GROUP, FEAT, HALF), BF16),
        pltpu.VMEM((FEAT, HALF), F32),
        pltpu.VMEM((FEAT, HALF), F32),
        pltpu.VMEM((FEAT, HALF), F32),
        pltpu.VMEM((FEAT, HALF), F32),
        pltpu.VMEM((STEPS, 2 * ROWS, FEAT), BF16),
        pltpu.VMEM((STEPS, ROWS, FEAT), BF16),
        pltpu.VMEM((STEPS, ROWS, FEAT), BF16),
        pltpu.VMEM((STEPS, 2, 64, FEAT), BF16),
        pltpu.VMEM((STEPS, 2, FEAT, FEAT), BF16),
        pltpu.VMEM((STEPS, 2, FEAT, FEAT), BF16),
        pltpu.VMEM((STEPS, FEAT, FEAT), BF16),
        pltpu.VMEM((STEPS, 3, 32, FEAT), BF16),
        pltpu.VMEM((STEPS, 32, FEAT), F32),
        pltpu.VMEM((STEPS, 16, FEAT), F32),
        pltpu.VMEM((2, STEPS, 2 * ROWS, FEAT), BF16),
        pltpu.VMEM((8, 128), F32),
        pltpu.VMEM((8, 128), F32),
        pltpu.SMEM((8, 128), F32),
        pltpu.SemaphoreType.DMA((MESSAGES, STEPS)),
        pltpu.SemaphoreType.DMA((MESSAGES, STEPS)),
        pltpu.SemaphoreType.DMA((3,)),
    ]
    att, gq, gk, gv = pl.pallas_call(
        kernel,
        out_shape=[jax.ShapeDtypeStruct((HALF, FEAT), BF16)] * 4,
        in_specs=[smem] * 4 + [vmem] * 9,
        out_specs=[vmem] * 4,
        scratch_shapes=scratch,
        compiler_params=pltpu.CompilerParams(
            collective_id=0, has_side_effects=True, vmem_limit_bytes=56 * 2**20
        ),
        name="fast_attention",
    )(
        frequency,
        directions,
        dir_weight,
        dir_mask,
        directions,
        queries,
        keys,
        values,
        cotangent,
        positions,
        species.reshape(1, ATOMS),
        domain.reshape(1, ATOMS),
        species_gain,
    )
    return att, gq, gk, gv


def solution(mesh):
    return jax.shard_map(
        per_device,
        mesh=mesh,
        in_specs=(
            P("atoms", None),
            P("atoms", None),
            P("atoms", None),
            P("atoms", None),
            P(None, "atoms"),
            P("atoms"),
            P("atoms"),
            P(),
            P(),
            P(None, "dirs"),
            P("dirs"),
            P("dirs"),
        ),
        out_specs=(
            P(("atoms", "dirs"), None),
            P(("atoms", "dirs"), None),
            P(("atoms", "dirs"), None),
            P(("atoms", "dirs"), None),
        ),
        check_vma=False,
    )
```

time: 111 us -> 107 us (0.964)
  Pallas kernels: 106 us -> 101 us
    pallas_call x1, Pallas kernels: 106 us -> 101 us  [per_device(): pl.pallas_call(kernel, out_shape=[jax.ShapeDtypeStruct((HALF, FEAT), BF16...]
where the time goes in v2:
time: 107 us
  Pallas kernels  101 us (94%)
  local copies, waits for them, and re-layouts  4.5 us (4%)
    pallas_call x1, Pallas kernels, per_device(): pl.pallas_call(kernel, out_shape=[jax.ShapeDtypeStruct((HALF, FEAT), BF16...  101 us
    unnamed x10, local copies, waits for them, and re-layouts  4.5 us

profile of v2, /device:TPU:1, one launch (start us, length us, event | category | flops | bytes accessed | tf_op | source)
XLA Modules:
  0.0 106.6 jit_solution(3161157647639317313)
XLA Ops:
  0.6 101.5 %fast_attention.1 = (bf16[1024,128]{1,0:T(8,128)(2,1)}, bf16[1024,128]{1,0:T(8,128)(2,1)}, bf16[1024,128]{1,0:T(8,128)(2,1)}, bf16[1024,128]{1,0:T(8,128)(2,1)}) custom-call(f32[32]{0:T(128)} %freq_ref.1, f32[3,44]{1,0:T(4,128)} %dirs_rows_ref.1, f32[44]{0:T(128)} %weight_ref.1, s32[44]{0:T(128)} %mask_ref.1, f32[3,44]{1,0:T(4,128)} %dirs_rows_ref.1, ...), custom_call_target="tpu_custom_call" | custom-call | tf_op jit(solution)/shard_map/fast_attention/pallas_call | solution.py:525
  102.1 0.0 copy-start.2
  102.1 1.7 %copy.20 = bf16[1024,128]{1,0:T(8,128)(2,1)} copy(bf16[1024,128]{1,0:T(8,128)(2,1)} %get-tuple-element.8) | data formatting | bytes 524288
  103.8 0.0 copy-done.2
  103.9 0.0 copy-start.1
  103.9 0.7 copy.21
  104.6 0.3 copy-done.1
  104.9 0.0 copy-start
  104.9 0.7 copy.22
  105.6 0.3 copy-done
  105.9 0.7 copy.23
Async XLA Ops:
  102.1 1.7 %copy-start.2 = (bf16[1024,128]{1,0:T(8,128)(2,1)S(1)}, bf16[1024,128]{1,0:T(8,128)(2,1)}, u32[]{:S(2)}) copy-start(bf16[1024,128]{1,0:T(8,128)(2,1)} %get-tuple-element.9) | copy-start | bytes 786436
  103.9 1.0 copy-start.1
  104.9 1.0 copy-start

commit v3 on v2

--- a/solution.py
+++ b/solution.py
@@ -1,4 +1,4 @@
-import functools
+import itertools
 import math
 
 import jax
@@ -36,10 +36,92 @@
     0.3106880275307806,
 )
 
-CORE_RS, RING_RS, HOP_RS, LINE_RS, Y_RS = 0, 1, 3, 5, 8
-Y_AG, LINE_AG, RING_AG, HOP_AG, CORE_AG = 9, 12, 15, 17, 19
-MESSAGES = 20
-STAGES = 11
+ORDERS = (('x', 'y', 'z'), ('z', 'y', 'x'))
+SIZE = {"c": 2, "x": 4, "z": 4, "y": 2}
+STAGES = 9
+FILL = 4
+TICKS = (
+    (),
+    ((0, 0),),
+    (),
+    ((0, 1), (1, 0)),
+    (),
+    ((1, 1), (2, 0)),
+    (),
+    ((2, 1), (3, 0)),
+    ((0, 2),),
+    ((3, 1), (4, 0)),
+    ((1, 2),),
+    ((4, 1), (5, 0)),
+    ((0, 3), (2, 2)),
+    ((5, 1), (6, 0)),
+    ((1, 3), (3, 2)),
+    ((6, 1), (7, 0)),
+    ((0, 4), (2, 3), (4, 2)),
+    ((7, 1), (8, 0)),
+    ((1, 4), (3, 3), (5, 2)),
+    ((8, 1), (9, 0)),
+    ((0, 5), (2, 4), (4, 3), (6, 2)),
+    ((9, 1), (10, 0)),
+    (),
+    ((1, 5), (3, 4), (5, 3), (7, 2)),
+    ((10, 1),),
+    ((0, 6), (2, 5), (4, 4), (6, 3), (8, 2)),
+    ((3, 5), (5, 4), (1, 6), (9, 2), (7, 3), (4, 5), (10, 2), (6, 4), (2, 6), (8, 3), (3, 6), (9, 3), (0, 7), (5, 5), (7, 4), (4, 6), (1, 7), (10, 3), (6, 5), (8, 4), (0, 8)),
+    (),
+    ((1, 8), (2, 7), (5, 6), (7, 5), (9, 4)),
+    ((3, 7), (6, 6), (8, 5), (10, 4)),
+    ((2, 8), (4, 7)),
+    ((3, 8), (9, 5)),
+    ((7, 6),),
+    ((4, 8), (5, 7), (8, 6), (10, 5)),
+    ((6, 7),),
+    ((5, 8), (9, 6)),
+    (),
+    ((6, 8), (10, 6)),
+    ((7, 7),),
+    ((8, 7),),
+    ((7, 8),),
+    ((9, 7),),
+    ((8, 8),),
+    ((10, 7),),
+    ((9, 8),),
+    (),
+    ((10, 8),),
+    (),
+)
+
+
+def levels_of(g):
+    levels, rows, taken, kept = [], 2 * ROWS, 0, 0
+    for axes in ("c",) + ORDERS[g % len(ORDERS)]:
+        count = math.prod(SIZE[axis] for axis in axes)
+        rows //= count
+        levels.append((axes, rows, taken, kept))
+        taken += (count - 1) * rows
+        kept += rows
+    return levels
+
+
+def offsets_of(axes, gather):
+    choices = []
+    for axis in axes:
+        if gather and axis == "y":
+            choices.append([{"y": h, "d": d} for h in range(2) for d in range(2)])
+        else:
+            choices.append([{axis: step} for step in range(SIZE[axis])])
+    merged = [{k: v for part in parts for k, v in part.items()} for parts in itertools.product(*choices)]
+    return [steps for steps in merged if any(steps.values())]
+
+
+def first_messages(g):
+    levels = levels_of(g)
+    counts = [len(offsets_of(axes, False)) for axes, _, _, _ in levels]
+    counts += [len(offsets_of(axes, True)) for axes, _, _, _ in levels[::-1]]
+    return [sum(counts[:n]) for n in range(len(counts) + 1)]
+
+
+MESSAGES = max(first_messages(g)[-1] for g in range(STEPS))
 
 
 def horner(coefficients, square):
@@ -89,7 +171,6 @@
     value_t,
     grad_t,
     cos_sin,
-    far_cos_sin,
     key_rot,
     query_rot,
     back_q,
@@ -99,15 +180,8 @@
     gq_acc,
     gk_acc,
     part,
-    core_in,
-    core_sum,
-    ring_in,
-    relay,
-    hop_in,
-    line_sum,
-    line_in,
-    y_sum,
-    y_in,
+    taken_in,
+    kept_sum,
     state,
     dirs_send,
     dirs_recv,
@@ -125,137 +199,102 @@
     near_base = dirs_at * HALF
     far_base = HALF - near_base
 
-    def along(at, step, stride):
-        return atoms_at + (lax.rem(at + step, 4) - at) * stride
-
-    other_core = {"atoms": atoms_at + 1 - 2 * core}
-    y_far = atoms_at + 32 - 64 * y_at
-    y_peers = [
-        {"atoms": y_far, "dirs": dirs_at},
-        {"atoms": atoms_at, "dirs": 1 - dirs_at},
-        {"atoms": y_far, "dirs": 1 - dirs_at},
-    ]
-
+    place = {"c": core, "x": x_at, "z": z_at, "y": y_at}
+
+    def device(steps):
+        at = {axis: lax.rem(place[axis] + steps.get(axis, 0), SIZE[axis]) for axis in place}
+        to = {"atoms": ((at["y"] * 4 + at["x"]) * 4 + at["z"]) * 2 + at["c"]}
+        if steps.get("d", 0):
+            to["dirs"] = 1 - dirs_at
+        return to
+
+    def part_of(axes, steps):
+        index = 0
+        for axis in axes:
+            index = index * SIZE[axis] + lax.rem(place[axis] + steps.get(axis, 0), SIZE[axis])
+        return index
+
+    met = []
+    for g in range(STEPS):
+        for axes, _, _, _ in levels_of(g):
+            met += [steps for steps in offsets_of(axes, True) if steps not in met]
+    met += [steps for steps in ({"d": 1},) if {"y": 0, "d": 1} not in met]
     barrier = pltpu.get_barrier_semaphore()
-    partners = [other_core] + y_peers
-    for step in range(1, 4):
-        partners += [{"atoms": along(x_at, step, 8)}, {"atoms": along(z_at, step, 2)}]
+    partners = [device(steps) for steps in met]
     for partner in partners:
         pl.semaphore_signal(
             barrier, inc=1, device_id=partner, device_id_type=pl.DeviceIdType.MESH
         )
 
-    core_row = core * ROWS
-
-    def place_of(g):
-        odd = lax.rem(g, 2)
-        first = x_at + odd * (z_at - x_at)
-        second = z_at + odd * (x_at - z_at)
-        return first, second, 8 - 6 * odd, 2 + 6 * odd
-
-    def rows_of(g, step):
-        first, _, _, _ = place_of(g)
-        return core_row + lax.rem(first + step, 4) * FEAT
-
-    def message(number, g):
-        first, second, first_stride, second_stride = place_of(g)
-        ahead = {"atoms": along(first, 1, first_stride)}
-        behind = {"atoms": along(first, 3, first_stride)}
-        first_row = core_row + first * FEAT
-        second_row = first_row + second * 32
-        y_row = second_row + y_at * 16
-        if number == CORE_RS:
-            src = part.at[g, tile_of((1 - core) * ROWS, ROWS, ROWS)]
-            dst, to = core_in.at[g], other_core
-        elif number < HOP_RS:
-            side = number - RING_RS
-            src = core_sum.at[g, tile_of(lax.rem(first + 2, 4) * FEAT + 64 * side, 64, 64)]
-            dst, to = ring_in.at[g, side], (ahead, behind)[side]
-        elif number < LINE_RS:
-            side = number - HOP_RS
-            src, dst, to = relay.at[g, side], hop_in.at[g, side], (ahead, behind)[side]
-        elif number < Y_RS:
-            step = number - LINE_RS + 1
-            src = line_sum.at[g, tile_of(lax.rem(second + step, 4) * 32, 32, 32)]
-            dst, to = line_in.at[g, 3 - step], {"atoms": along(second, step, second_stride)}
-        elif number == Y_RS:
-            src = y_sum.at[g, tile_of((1 - y_at) * 16, 16, 16)]
-            dst, to = y_in.at[g], y_peers[0]
-        elif number < LINE_AG:
-            src = dst = state.at[dirs_at, g, tile_of(y_row, 16, 16)]
-            to = y_peers[number - Y_AG]
-        elif number < RING_AG:
-            src = dst = state.at[:, g, tile_of(second_row, 32, 32)]
-            to = {"atoms": along(second, number - LINE_AG + 1, second_stride)}
-        elif number < HOP_AG:
-            src = dst = state.at[:, g, tile_of(first_row, FEAT, FEAT)]
-            to = (ahead, behind)[number - RING_AG]
-        elif number < CORE_AG:
-            side = number - HOP_AG
-            src = dst = state.at[:, g, tile_of(rows_of(g, (3, 1)[side]) + 64 * side, 64, 64)]
-            to = (ahead, behind)[side]
+    def state_rows(g, level):
+        start = 0
+        for axes, rows, _, _ in levels_of(g)[: level + 1]:
+            start = start + part_of(axes, {}) * rows
+        rows = levels_of(g)[level][1]
+        return tile_of(start, rows, rows)
+
+    def messages(number, g):
+        levels = levels_of(g)
+        first = first_messages(g)[number]
+        result = []
+        if number < len(levels):
+            axes, rows, taken, _ = levels[number]
+            for n, steps in enumerate(offsets_of(axes, False)):
+                start = part_of(axes, steps) * rows
+                if number == 0:
+                    src = part.at[g, tile_of(start, rows, rows)]
+                else:
+                    src = kept_sum.at[g, tile_of(levels[number - 1][3] + start, rows, rows)]
+                dst = taken_in.at[g, taken + n * rows : taken + (n + 1) * rows]
+                result.append((src, dst, steps))
         else:
-            src = dst = state.at[:, g, tile_of(core_row, ROWS, ROWS)]
-            to = other_core
-        return pltpu.make_async_remote_copy(
-            src_ref=src,
-            dst_ref=dst,
-            send_sem=send_sem.at[number, g],
-            recv_sem=recv_sem.at[number, g],
-            device_id=to,
-            device_id_type=pl.DeviceIdType.MESH,
-        )
-
-    first_of = (
-        CORE_RS, RING_RS, HOP_RS, LINE_RS, Y_RS, Y_AG, LINE_AG, RING_AG, HOP_AG, CORE_AG, MESSAGES
-    )
+            level = 2 * len(levels) - 1 - number
+            whole = any("y" in axes for axes, _, _, _ in levels[level + 1 :])
+            here = state.at[slice(None) if whole else dirs_at, g, state_rows(g, level)]
+            result = [(here, here, steps) for steps in offsets_of(levels[level][0], True)]
+        return [
+            pltpu.make_async_remote_copy(
+                src_ref=src,
+                dst_ref=dst,
+                send_sem=send_sem.at[g, first + n],
+                recv_sem=recv_sem.at[g, first + n],
+                device_id=device(steps),
+                device_id_type=pl.DeviceIdType.MESH,
+            )
+            for n, (src, dst, steps) in enumerate(result)
+        ]
 
     def stage(number, g):
+        levels = levels_of(g)
+        depth = len(levels)
         if number > 0:
-            for n in range(first_of[number - 1], first_of[number]):
-                message(n, g).wait()
-        if number == 1:
-            mine = part[g, tile_of(core_row, ROWS, ROWS), :].astype(F32)
-            core_sum[g] = (mine + core_in[g].astype(F32)).astype(BF16)
-        elif number == 2:
-            for side, step in ((0, 1), (1, 3)):
-                rows = lax.rem(place_of(g)[0] + step, 4) * FEAT
-                met, kept = rows + 64 * side, rows + 64 * (1 - side)
-                total = core_sum[g, tile_of(met, 64, 64), :].astype(F32)
-                total = total + ring_in[g, side].astype(F32)
-                relay[g, side, 64 * side : 64 * side + 64, :] = total.astype(BF16)
-                relay[g, side, 64 * (1 - side) : 64 * (1 - side) + 64, :] = core_sum[
-                    g, tile_of(kept, 64, 64), :
-                ]
-        elif number == 3:
-            total = core_sum[g, tile_of(place_of(g)[0] * FEAT, FEAT, FEAT), :].astype(F32)
-            total = total + hop_in[g, 0].astype(F32) + hop_in[g, 1].astype(F32)
-            line_sum[g] = total.astype(BF16)
-        elif number == 4:
-            total = line_sum[g, tile_of(place_of(g)[1] * 32, 32, 32), :].astype(F32)
-            for slot in range(3):
-                total = total + line_in[g, slot].astype(F32)
-            y_sum[g] = total
-        elif number == 5:
-            first, second, _, _ = place_of(g)
-            row = core_row + first * FEAT + second * 32 + y_at * 16
-            total = y_sum[g, tile_of(y_at * 16, 16, 16), :] + y_in[g]
-            state[dirs_at, g, tile_of(row, 16, 16), :] = total.astype(BF16)
-        if number < STAGES - 1:
-            for n in range(first_of[number], first_of[number + 1]):
-                message(n, g).start()
-
-    def exchange(t, lowest, highest):
-        for number in range(STAGES - 1, -1, -1):
-            if highest < number or lowest - number >= STEPS:
-                continue
-            if lowest >= number and highest - number < STEPS:
-                stage(number, t - number)
+            for copy in messages(number - 1, g):
+                copy.wait()
+        if 0 < number <= depth:
+            axes, rows, taken, kept = levels[number - 1]
+            start = part_of(axes, {}) * rows
+            if number == 1:
+                total = part[g, tile_of(start, rows, rows), :].astype(F32)
             else:
-
-                @pl.when(jnp.logical_and(t >= number, t < number + STEPS))
-                def _(number=number):
-                    stage(number, t - number)
+                total = kept_sum[g, tile_of(levels[number - 2][3] + start, rows, rows), :].astype(F32)
+            for n in range(math.prod(SIZE[axis] for axis in axes) - 1):
+                total = total + taken_in[g, taken + n * rows : taken + (n + 1) * rows, :].astype(F32)
+            if number == depth:
+                state[dirs_at, g, state_rows(g, depth - 1), :] = total.astype(BF16)
+            else:
+                kept_sum[g, kept : kept + rows, :] = total.astype(BF16)
+        if number < 2 * depth:
+            for copy in messages(number, g):
+                copy.start()
+
+    def exchange(t, ticks):
+        for tick in ticks:
+            if TICKS[tick]:
+
+                @pl.when(t == tick)
+                def _(tick=tick):
+                    for g, number in TICKS[tick]:
+                        stage(number, g)
 
     dirs_send[...] = jnp.zeros_like(dirs_send)
     dirs_send[0:3, 0:DIRS] = dirs_rows_ref[...]
@@ -323,6 +362,8 @@
 
     def state_step(i):
         for u in range(GROUP):
+            if u == GROUP // 2:
+                exchange(2 * i, range(0, 2 * STEPS, 2))
             at = i * GROUP + u
             for low in range(0, ATOMS, WIDTH):
                 columns = pl.ds(low, WIDTH)
@@ -346,32 +387,27 @@
                     product[u * FEAT : (u + 1) * FEAT] * coef(i * GROUP + u)
                 ).astype(BF16)
 
+    def far_angles(at):
+        for low in range(0, HALF, WIDTH):
+            columns = pl.ds(low, WIDTH)
+            for low_f, cosine, sine in angles(far_dirs, at, columns):
+                cos_sin[DIRS + at, 0, low_f : low_f + 16, columns] = cosine
+                cos_sin[DIRS + at, 1, low_f : low_f + 16, columns] = sine
+
     def output_step(i, far):
         low_at = far * HALF
+        table_at = far * DIRS + i * GROUP
         for u in range(GROUP):
-            at = i * GROUP + u
             for low in range(0, HALF, WIDTH):
                 columns = pl.ds(low, WIDTH)
-                if far:
-                    table = angles(far_dirs, at, columns)
-                else:
-                    table = (
-                        (
-                            low_f,
-                            cos_sin[at, 0, low_f : low_f + 16, columns],
-                            cos_sin[at, 1, low_f : low_f + 16, columns],
-                        )
-                        for low_f in range(0, FREQS, 16)
-                    )
-                for low_f, cosine, sine in table:
-                    if far:
-                        far_cos_sin[u, 0, low_f : low_f + 16, columns] = cosine
-                        far_cos_sin[u, 1, low_f : low_f + 16, columns] = sine
+                place = pl.ds(low_at + low, WIDTH)
+                for low_f in range(0, FREQS, 16):
+                    cosine = cos_sin[table_at + u, 0, low_f : low_f + 16, columns]
+                    sine = cos_sin[table_at + u, 1, low_f : low_f + 16, columns]
                     for p in (low_f, low_f + FREQS):
                         for x_ref, y_ref in ((key_t, key_rot), (query_t, query_rot)):
                             lead = x_ref[p : p + 16, columns]
                             trail = x_ref[p + 64 : p + 80, columns]
-                            place = pl.ds(low_at + low, WIDTH)
                             y_ref[u, p : p + 16, place] = lead * cosine - trail * sine
                             y_ref[u, p + 64 : p + 80, place] = lead * sine + trail * cosine
         owner = 1 - dirs_at if far else dirs_at
@@ -396,12 +432,9 @@
         for low in range(0, HALF, WIDTH):
             columns = pl.ds(low, WIDTH)
             for low_f in range(0, FREQS, 16):
-                if far:
-                    tables = [far_cos_sin[u, :, low_f : low_f + 16, columns] for u in range(GROUP)]
-                else:
-                    tables = [
-                        cos_sin[i * GROUP + u, :, low_f : low_f + 16, columns] for u in range(GROUP)
-                    ]
+                tables = [
+                    cos_sin[table_at + u, :, low_f : low_f + 16, columns] for u in range(GROUP)
+                ]
                 for p in (low_f, low_f + FREQS):
                     for back, total in ((back_q, gq_acc), (back_k, gk_acc)):
                         lead_sum = trail_sum = None
@@ -427,14 +460,14 @@
         dst_ref=dirs_recv,
         send_sem=dirs_sem.at[0],
         recv_sem=dirs_sem.at[1],
-        device_id=y_peers[1],
+        device_id={"dirs": 1 - dirs_at},
         device_id_type=pl.DeviceIdType.MESH,
     )
     dirs_copy.start()
 
-    def first_loop(t, carry):
-        state_step(t)
-        exchange(t, 0, STEPS - 1)
+    def first_loop(i, carry):
+        state_step(i)
+        exchange(2 * i + 1, range(1, 2 * STEPS, 2))
         return carry
 
     lax.fori_loop(0, STEPS, first_loop, 0)
@@ -444,10 +477,22 @@
     to_scalars.start()
     to_scalars.wait()
 
+    def fill_loop(t, carry):
+        exchange(t + 2 * STEPS, range(2 * STEPS, 2 * STEPS + FILL))
+
+        def fill(n, inner):
+            far_angles(t * (DIRS // FILL) + n)
+            return inner
+
+        return lax.fori_loop(0, DIRS // FILL, fill, carry)
+
+    lax.fori_loop(0, FILL, fill_loop, 0)
+
     def second_loop(i, carry):
-        exchange(i + STEPS, STEPS, 2 * STEPS - 1)
-        output_step(i, 0)
-        output_step(i, 1)
+        at = 2 * STEPS + FILL
+        for far in range(2):
+            exchange(at + 2 * i + far, range(at + far, at + 2 * STEPS, 2))
+            output_step(i, far)
         return carry
 
     lax.fori_loop(0, STEPS, second_loop, 0)
@@ -494,8 +539,7 @@
         pltpu.VMEM((FEAT, ATOMS), BF16),
         pltpu.VMEM((FEAT, HALF), BF16),
         pltpu.VMEM((FEAT, HALF), BF16),
-        pltpu.VMEM((DIRS, 2, FREQS, HALF), BF16),
-        pltpu.VMEM((GROUP, 2, FREQS, HALF), BF16),
+        pltpu.VMEM((2 * DIRS, 2, FREQS, HALF), BF16),
         pltpu.VMEM((GROUP, FEAT, ATOMS), BF16),
         pltpu.VMEM((GROUP, FEAT, ATOMS), BF16),
         pltpu.VMEM((2, GROUP, FEAT, HALF), BF16),
@@ -505,21 +549,14 @@
         pltpu.VMEM((FEAT, HALF), F32),
         pltpu.VMEM((FEAT, HALF), F32),
         pltpu.VMEM((STEPS, 2 * ROWS, FEAT), BF16),
-        pltpu.VMEM((STEPS, ROWS, FEAT), BF16),
-        pltpu.VMEM((STEPS, ROWS, FEAT), BF16),
-        pltpu.VMEM((STEPS, 2, 64, FEAT), BF16),
-        pltpu.VMEM((STEPS, 2, FEAT, FEAT), BF16),
-        pltpu.VMEM((STEPS, 2, FEAT, FEAT), BF16),
-        pltpu.VMEM((STEPS, FEAT, FEAT), BF16),
-        pltpu.VMEM((STEPS, 3, 32, FEAT), BF16),
-        pltpu.VMEM((STEPS, 32, FEAT), F32),
-        pltpu.VMEM((STEPS, 16, FEAT), F32),
+        pltpu.VMEM((STEPS, 2 * ROWS, FEAT), BF16),
+        pltpu.VMEM((STEPS, 2 * ROWS, FEAT), BF16),
         pltpu.VMEM((2, STEPS, 2 * ROWS, FEAT), BF16),
         pltpu.VMEM((8, 128), F32),
         pltpu.VMEM((8, 128), F32),
         pltpu.SMEM((8, 128), F32),
-        pltpu.SemaphoreType.DMA((MESSAGES, STEPS)),
-        pltpu.SemaphoreType.DMA((MESSAGES, STEPS)),
+        pltpu.SemaphoreType.DMA((STEPS, MESSAGES)),
+        pltpu.SemaphoreType.DMA((STEPS, MESSAGES)),
         pltpu.SemaphoreType.DMA((3,)),
     ]
     att, gq, gk, gv = pl.pallas_call(

time: 107 us -> 89.3 us (0.83)
  Pallas kernels: 101 us -> 83.4 us
    pallas_call x1, Pallas kernels: 101 us -> 83.4 us  [per_device(): pl.pallas_call(kernel, out_shape=[jax.ShapeDtypeStruct((HALF, FEAT), BF16...]
where the time goes in v3:
time: 89.3 us; the launch traced here: 88.6 us
  Pallas kernels  83.4 us (93%)
  local copies, waits for them, and re-layouts  4.5 us (5%)
    pallas_call x1, Pallas kernels, per_device(): pl.pallas_call(kernel, out_shape=[jax.ShapeDtypeStruct((HALF, FEAT), BF16...  83.4 us
    unnamed x10, local copies, waits for them, and re-layouts  4.5 us

profile of v3, /device:TPU:1, one launch (start us, length us, event | category | flops | bytes accessed | tf_op | source)
XLA Modules:
  0.0 88.6 jit_solution(37196456302380964)
XLA Ops:
  0.6 83.4 %fast_attention.1 = (bf16[1024,128]{1,0:T(8,128)(2,1)}, bf16[1024,128]{1,0:T(8,128)(2,1)}, bf16[1024,128]{1,0:T(8,128)(2,1)}, bf16[1024,128]{1,0:T(8,128)(2,1)}) custom-call(f32[32]{0:T(128)} %freq_ref.1, f32[3,44]{1,0:T(4,128)} %dirs_rows_ref.1, f32[44]{0:T(128)} %weight_ref.1, s32[44]{0:T(128)} %mask_ref.1, f32[3,44]{1,0:T(4,128)} %dirs_rows_ref.1, ...), custom_call_target="tpu_custom_call" | custom-call | tf_op jit(solution)/shard_map/fast_attention/pallas_call | solution.py:562
  84.1 0.0 copy-start.2
  84.1 1.7 %copy.20 = bf16[1024,128]{1,0:T(8,128)(2,1)} copy(bf16[1024,128]{1,0:T(8,128)(2,1)} %get-tuple-element.8) | data formatting | bytes 524288
  85.8 0.0 copy-done.2
  85.8 0.0 copy-start.1
  85.8 0.7 copy.21
  86.5 0.3 copy-done.1
  86.8 0.0 copy-start
  86.8 0.7 copy.22
  87.5 0.3 copy-done
  87.9 0.7 copy.23
Async XLA Ops:
  84.1 1.7 %copy-start.2 = (bf16[1024,128]{1,0:T(8,128)(2,1)S(1)}, bf16[1024,128]{1,0:T(8,128)(2,1)}, u32[]{:S(2)}) copy-start(bf16[1024,128]{1,0:T(8,128)(2,1)} %get-tuple-element.9) | copy-start | bytes 786436
  85.8 1.0 %copy-start.1 = (bf16[1024,128]{1,0:T(8,128)(2,1)S(1)}, bf16[1024,128]{1,0:T(8,128)(2,1)}, u32[]{:S(2)}) copy-start(bf16[1024,128]{1,0:T(8,128)(2,1)} %get-tuple-element.10) | copy-start | bytes 786436
  86.8 1.0 %copy-start = (bf16[1024,128]{1,0:T(8,128)(2,1)S(1)}, bf16[1024,128]{1,0:T(8,128)(2,1)}, u32[]{:S(2)}) copy-start(bf16[1024,128]{1,0:T(8,128)(2,1)} %get-tuple-element.11) | copy-start | bytes 786436

commit v4 on v3

--- a/solution.py
+++ b/solution.py
@@ -21,20 +21,8 @@
 ROWS = GROUP * FEAT
 WIDTH = 256
 
-SINE = (
-    4.442882919124345,
-    -7.3082456865090855,
-    3.606354218433185,
-    -0.8461116503751638,
-    0.10982451642692614,
-)
-COSINE = (
-    1.4142134962552289,
-    -6.978850948563847,
-    5.739460376907657,
-    -1.8835579059891776,
-    0.3106880275307806,
-)
+SINE = (4.4428795675460835, -7.307816684491783, 3.59777417808721, -0.791199392161295)
+COSINE = (1.4142040148090755, -6.977637323456294, 5.715187874756719, -1.7282138922235275)
 
 ORDERS = (('x', 'y', 'z'), ('z', 'y', 'x'))
 SIZE = {"c": 2, "x": 4, "z": 4, "y": 2}
@@ -60,34 +48,34 @@
     ((0, 4), (2, 3), (4, 2)),
     ((7, 1), (8, 0)),
     ((1, 4), (3, 3), (5, 2)),
-    ((8, 1), (9, 0)),
-    ((0, 5), (2, 4), (4, 3), (6, 2)),
-    ((9, 1), (10, 0)),
-    (),
-    ((1, 5), (3, 4), (5, 3), (7, 2)),
-    ((10, 1),),
-    ((0, 6), (2, 5), (4, 4), (6, 3), (8, 2)),
-    ((3, 5), (5, 4), (1, 6), (9, 2), (7, 3), (4, 5), (10, 2), (6, 4), (2, 6), (8, 3), (3, 6), (9, 3), (0, 7), (5, 5), (7, 4), (4, 6), (1, 7), (10, 3), (6, 5), (8, 4), (0, 8)),
-    (),
-    ((1, 8), (2, 7), (5, 6), (7, 5), (9, 4)),
-    ((3, 7), (6, 6), (8, 5), (10, 4)),
-    ((2, 8), (4, 7)),
-    ((3, 8), (9, 5)),
+    ((0, 5), (6, 2), (8, 1), (9, 0)),
+    ((2, 4), (4, 3)),
+    ((1, 5), (3, 4), (7, 2), (9, 1), (10, 0)),
+    ((5, 3),),
+    ((0, 6), (6, 3), (10, 1)),
+    ((2, 5), (3, 5), (4, 4), (8, 2)),
+    ((1, 6), (5, 4), (7, 3), (9, 2)),
+    ((6, 4), (4, 5), (2, 6), (0, 7), (3, 6), (8, 3), (9, 3), (10, 2), (5, 5), (7, 4), (0, 8)),
+    ((1, 7), (4, 6), (6, 5)),
+    ((10, 3), (2, 7), (9, 4), (1, 8)),
+    ((3, 7), (5, 6), (7, 5), (8, 4)),
+    ((2, 8), (6, 6), (10, 4)),
+    ((3, 8), (4, 7), (9, 5)),
     ((7, 6),),
-    ((4, 8), (5, 7), (8, 6), (10, 5)),
-    ((6, 7),),
-    ((5, 8), (9, 6)),
-    (),
-    ((6, 8), (10, 6)),
-    ((7, 7),),
-    ((8, 7),),
+    ((4, 8), (5, 7), (8, 5), (10, 5)),
+    ((6, 7), (9, 6)),
+    ((5, 8),),
+    ((6, 8), (7, 7), (8, 6), (10, 6)),
+    (),
     ((7, 8),),
     ((9, 7),),
-    ((8, 8),),
-    ((10, 7),),
-    ((9, 8),),
+    (),
+    ((8, 7), (9, 8)),
+    ((10, 7), (8, 8)),
     (),
     ((10, 8),),
+    (),
+    (),
     (),
 )
 
@@ -132,8 +120,7 @@
 
 
 def cos_sin_turns(turns):
-    nearest = (turns + 12582912.0) - 12582912.0
-    rest = turns - nearest
+    rest = turns - jnp.round(turns)
     square = rest * rest
     sine = horner(SINE, square) * rest
     cosine = horner(COSINE, square)
@@ -507,10 +494,20 @@
             whole = total[:, place]
             if factor is not None:
                 whole = whole * factor
-            out[place, :] = whole.T.astype(BF16)
+            out[:, place] = whole.astype(BF16)
         return carry
 
     lax.fori_loop(0, HALF // 128, finish, 0)
+
+
+def turn_kernel(*refs):
+    def turn(block, carry):
+        rows = tile_of(block * 128, 128, 128)
+        for source, result in zip(refs[:4], refs[4:]):
+            result[rows, :] = source[:, rows].astype(F32).T.astype(BF16)
+        return carry
+
+    lax.fori_loop(0, HALF // 128, turn, 0)
 
 
 def per_device(
@@ -559,9 +556,9 @@
         pltpu.SemaphoreType.DMA((STEPS, MESSAGES)),
         pltpu.SemaphoreType.DMA((3,)),
     ]
-    att, gq, gk, gv = pl.pallas_call(
+    turned = pl.pallas_call(
         kernel,
-        out_shape=[jax.ShapeDtypeStruct((HALF, FEAT), BF16)] * 4,
+        out_shape=[jax.ShapeDtypeStruct((FEAT, HALF), BF16)] * 4,
         in_specs=[smem] * 4 + [vmem] * 9,
         out_specs=[vmem] * 4,
         scratch_shapes=scratch,
@@ -584,7 +581,15 @@
         domain.reshape(1, ATOMS),
         species_gain,
     )
-    return att, gq, gk, gv
+    return tuple(
+        pl.pallas_call(
+            turn_kernel,
+            out_shape=[jax.ShapeDtypeStruct((HALF, FEAT), BF16)] * 4,
+            in_specs=[vmem] * 4,
+            out_specs=[vmem] * 4,
+            name="turn_results",
+        )(*turned)
+    )
 
 
 def solution(mesh):

time: 89.3 us -> 85 us (0.952)
  local copies, waits for them, and re-layouts: 4.5 us -> 0 us
    unnamed x10 -> x0, local copies, waits for them, and re-layouts: 4.5 us -> none
    pallas_call x1 -> x2, Pallas kernels: 83.4 us -> 84.1 us  [the longest x1 81.2 us: per_device(): pl.pallas_call(kernel, out_shape=[jax.ShapeDtypeStruct((FEAT, HALF), BF16...]
where the time goes in v4:
time: 85 us; the launch traced here: 84.8 us
  Pallas kernels  84.1 us (99%)
    pallas_call x1, Pallas kernels, per_device(): pl.pallas_call(kernel, out_shape=[jax.ShapeDtypeStruct((FEAT, HALF), BF16...  81.2 us
    pallas_call x1, Pallas kernels, per_device(): pl.pallas_call(turn_kernel, out_shape=[jax.ShapeDtypeStruct((HALF, FEAT),...  3 us

profile of v4, /device:TPU:1, one launch (start us, length us, event | category | flops | bytes accessed | tf_op | source)
XLA Modules:
  0.0 84.8 jit_solution(4137933703470766738)
XLA Ops:
  0.6 81.2 %fast_attention.1 = (bf16[128,1024]{1,0:T(8,128)(2,1)}, bf16[128,1024]{1,0:T(8,128)(2,1)}, bf16[128,1024]{1,0:T(8,128)(2,1)}, bf16[128,1024]{1,0:T(8,128)(2,1)}) custom-call(f32[32]{0:T(128)} %freq_ref.1, f32[3,44]{1,0:T(4,128)} %dirs_rows_ref.1, f32[44]{0:T(128)} %weight_ref.1, s32[44]{0:T(128)} %mask_ref.1, f32[3,44]{1,0:T(4,128)} %dirs_rows_ref.1, ...), custom_call_target="tpu_custom_call" | custom-call | tf_op jit(solution)/shard_map/fast_attention/pallas_call | solution.py:559
  81.8 3.0 %turn_results.1 = (bf16[1024,128]{1,0:T(8,128)(2,1)}, bf16[1024,128]{1,0:T(8,128)(2,1)}, bf16[1024,128]{1,0:T(8,128)(2,1)}, bf16[1024,128]{1,0:T(8,128)(2,1)}) custom-call(bf16[128,1024]{1,0:T(8,128)(2,1)} %get-tuple-element.8.refs_0_, bf16[128,1024]{1,0:T(8,128)(2,1)} %get-tuple-element.9.refs_1_, bf16[128,1024]{1,0:T(8,128)(2,1)} %get-tuple-element.10.refs_2_, ...), custom_call_target="tpu_custom_call" | custom-call | tf_op jit(solution)/shard_map/turn_results/pallas_call | solution.py:585

commit v5 on v4

--- a/solution.py
+++ b/solution.py
@@ -100,16 +100,6 @@
             choices.append([{axis: step} for step in range(SIZE[axis])])
     merged = [{k: v for part in parts for k, v in part.items()} for parts in itertools.product(*choices)]
     return [steps for steps in merged if any(steps.values())]
-
-
-def first_messages(g):
-    levels = levels_of(g)
-    counts = [len(offsets_of(axes, False)) for axes, _, _, _ in levels]
-    counts += [len(offsets_of(axes, True)) for axes, _, _, _ in levels[::-1]]
-    return [sum(counts[:n]) for n in range(len(counts) + 1)]
-
-
-MESSAGES = max(first_messages(g)[-1] for g in range(STEPS))
 
 
 def horner(coefficients, square):
@@ -222,7 +212,6 @@
 
     def messages(number, g):
         levels = levels_of(g)
-        first = first_messages(g)[number]
         result = []
         if number < len(levels):
             axes, rows, taken, _ = levels[number]
@@ -243,20 +232,31 @@
             pltpu.make_async_remote_copy(
                 src_ref=src,
                 dst_ref=dst,
-                send_sem=send_sem.at[g, first + n],
-                recv_sem=recv_sem.at[g, first + n],
+                send_sem=send_sem.at[g, number],
+                recv_sem=recv_sem.at[g, number],
                 device_id=device(steps),
                 device_id_type=pl.DeviceIdType.MESH,
             )
-            for n, (src, dst, steps) in enumerate(result)
+            for src, dst, steps in result
         ]
+
+    def all_bytes(number, g):
+        levels = levels_of(g)
+        if number < len(levels):
+            axes, rows, taken, _ = levels[number]
+            return taken_in.at[g, taken : taken + len(offsets_of(axes, False)) * rows]
+        level = 2 * len(levels) - 1 - number
+        axes, rows, _, _ = levels[level]
+        whole = any("y" in others for others, _, _, _ in levels[level + 1 :])
+        return state.at[slice(None) if whole else 0, g, : len(offsets_of(axes, True)) * rows]
 
     def stage(number, g):
         levels = levels_of(g)
         depth = len(levels)
         if number > 0:
-            for copy in messages(number - 1, g):
-                copy.wait()
+            total = all_bytes(number - 1, g)
+            for sem in (send_sem, recv_sem):
+                pltpu.make_async_copy(total, total, sem.at[g, number - 1]).wait()
         if 0 < number <= depth:
             axes, rows, taken, kept = levels[number - 1]
             start = part_of(axes, {}) * rows
@@ -504,7 +504,7 @@
     def turn(block, carry):
         rows = tile_of(block * 128, 128, 128)
         for source, result in zip(refs[:4], refs[4:]):
-            result[rows, :] = source[:, rows].astype(F32).T.astype(BF16)
+            result[rows, :] = source[:, rows].T
         return carry
 
     lax.fori_loop(0, HALF // 128, turn, 0)
@@ -552,8 +552,8 @@
         pltpu.VMEM((8, 128), F32),
         pltpu.VMEM((8, 128), F32),
         pltpu.SMEM((8, 128), F32),
-        pltpu.SemaphoreType.DMA((STEPS, MESSAGES)),
-        pltpu.SemaphoreType.DMA((STEPS, MESSAGES)),
+        pltpu.SemaphoreType.DMA((STEPS, STAGES - 1)),
+        pltpu.SemaphoreType.DMA((STEPS, STAGES - 1)),
         pltpu.SemaphoreType.DMA((3,)),
     ]
     turned = pl.pallas_call(

time: 85 us -> 83 us (0.976)
  Pallas kernels: 84.1 us -> 82.2 us
    pallas_call x1, Pallas kernels: 81.2 us -> 79.4 us  [per_device(): pl.pallas_call(kernel, out_shape=[jax.ShapeDtypeStruct((FEAT, HALF), BF16...]
where the time goes in v5:
time: 83 us; the launch traced here: 82.9 us
  Pallas kernels  82.2 us (99%)
    pallas_call x1, Pallas kernels, per_device(): pl.pallas_call(kernel, out_shape=[jax.ShapeDtypeStruct((FEAT, HALF), BF16...  79.4 us
    pallas_call x1, Pallas kernels, per_device(): pl.pallas_call(turn_kernel, out_shape=[jax.ShapeDtypeStruct((HALF, FEAT),...  2.86 us

profile of v5, /device:TPU:1, one launch (start us, length us, event | category | flops | bytes accessed | tf_op | source)
XLA Modules:
  0.0 82.9 jit_solution(407460949647368106)
XLA Ops:
  0.6 79.4 %fast_attention.1 = (bf16[128,1024]{1,0:T(8,128)(2,1)}, bf16[128,1024]{1,0:T(8,128)(2,1)}, bf16[128,1024]{1,0:T(8,128)(2,1)}, bf16[128,1024]{1,0:T(8,128)(2,1)}) custom-call(f32[32]{0:T(128)} %freq_ref.1, f32[3,44]{1,0:T(4,128)} %dirs_rows_ref.1, f32[44]{0:T(128)} %weight_ref.1, s32[44]{0:T(128)} %mask_ref.1, f32[3,44]{1,0:T(4,128)} %dirs_rows_ref.1, ...), custom_call_target="tpu_custom_call" | custom-call | tf_op jit(solution)/shard_map/fast_attention/pallas_call | solution.py:559
  80.0 2.9 %turn_results.1 = (bf16[1024,128]{1,0:T(8,128)(2,1)}, bf16[1024,128]{1,0:T(8,128)(2,1)}, bf16[1024,128]{1,0:T(8,128)(2,1)}, bf16[1024,128]{1,0:T(8,128)(2,1)}) custom-call(bf16[128,1024]{1,0:T(8,128)(2,1)} %get-tuple-element.8.refs_0_, bf16[128,1024]{1,0:T(8,128)(2,1)} %get-tuple-element.9.refs_1_, bf16[128,1024]{1,0:T(8,128)(2,1)} %get-tuple-element.10.refs_2_, ...), custom_call_target="tpu_custom_call" | custom-call | tf_op jit(solution)/shard_map/turn_results/pallas_call | solution.py:585

commit v6 on v5

--- a/solution.py
+++ b/solution.py
@@ -347,9 +347,30 @@
             sine = jnp.concatenate([pairs[0][1], pairs[1][1]], axis=0).astype(BF16)
             yield low_f, cosine, sine
 
+    dirs_copy = pltpu.make_async_remote_copy(
+        src_ref=dirs_send,
+        dst_ref=dirs_recv,
+        send_sem=dirs_sem.at[0],
+        recv_sem=dirs_sem.at[1],
+        device_id={"dirs": 1 - dirs_at},
+        device_id_type=pl.DeviceIdType.MESH,
+    )
+    to_scalars = pltpu.make_async_copy(dirs_recv, far_dirs, dirs_sem.at[2])
+
     def state_step(i):
         for u in range(GROUP):
             if u == GROUP // 2:
+
+                @pl.when(i == 0)
+                def _():
+                    pl.semaphore_wait(barrier, len(partners))
+                    dirs_copy.start()
+
+                @pl.when(i == STEPS - 1)
+                def _():
+                    dirs_copy.wait()
+                    to_scalars.start()
+
                 exchange(2 * i, range(0, 2 * STEPS, 2))
             at = i * GROUP + u
             for low in range(0, ATOMS, WIDTH):
@@ -440,18 +461,6 @@
     for total in totals:
         total[...] = jnp.zeros_like(total)
 
-    pl.semaphore_wait(barrier, len(partners))
-
-    dirs_copy = pltpu.make_async_remote_copy(
-        src_ref=dirs_send,
-        dst_ref=dirs_recv,
-        send_sem=dirs_sem.at[0],
-        recv_sem=dirs_sem.at[1],
-        device_id={"dirs": 1 - dirs_at},
-        device_id_type=pl.DeviceIdType.MESH,
-    )
-    dirs_copy.start()
-
     def first_loop(i, carry):
         state_step(i)
         exchange(2 * i + 1, range(1, 2 * STEPS, 2))
@@ -459,9 +468,6 @@
 
     lax.fori_loop(0, STEPS, first_loop, 0)
 
-    dirs_copy.wait()
-    to_scalars = pltpu.make_async_copy(dirs_recv, far_dirs, dirs_sem.at[2])
-    to_scalars.start()
     to_scalars.wait()
 
     def fill_loop(t, carry):

time: 83 us -> 82.5 us (level)
  no operation moved by 1% of the time
where the time goes in v6:
time: 82.5 us; the launch traced here: 82.3 us
  Pallas kernels  81.7 us (99%)
    pallas_call x1, Pallas kernels, per_device(): pl.pallas_call(kernel, out_shape=[jax.ShapeDtypeStruct((FEAT, HALF), BF16...  78.8 us
    pallas_call x1, Pallas kernels, per_device(): pl.pallas_call(turn_kernel, out_shape=[jax.ShapeDtypeStruct((HALF, FEAT),...  2.86 us

profile of v6, /device:TPU:1, one launch (start us, length us, event | category | flops | bytes accessed | tf_op | source)
XLA Modules:
  0.0 82.3 jit_solution(7137239963155215034)
XLA Ops:
  0.6 78.8 %fast_attention.1 = (bf16[128,1024]{1,0:T(8,128)(2,1)}, bf16[128,1024]{1,0:T(8,128)(2,1)}, bf16[128,1024]{1,0:T(8,128)(2,1)}, bf16[128,1024]{1,0:T(8,128)(2,1)}) custom-call(f32[32]{0:T(128)} %freq_ref.1, f32[3,44]{1,0:T(4,128)} %dirs_rows_ref.1, f32[44]{0:T(128)} %weight_ref.1, s32[44]{0:T(128)} %mask_ref.1, f32[3,44]{1,0:T(4,128)} %dirs_rows_ref.1, ...), custom_call_target="tpu_custom_call" | custom-call | tf_op jit(solution)/shard_map/fast_attention/pallas_call | solution.py:565
  79.4 2.9 %turn_results.1 = (bf16[1024,128]{1,0:T(8,128)(2,1)}, bf16[1024,128]{1,0:T(8,128)(2,1)}, bf16[1024,128]{1,0:T(8,128)(2,1)}, bf16[1024,128]{1,0:T(8,128)(2,1)}) custom-call(bf16[128,1024]{1,0:T(8,128)(2,1)} %get-tuple-element.8.refs_0_, bf16[128,1024]{1,0:T(8,128)(2,1)} %get-tuple-element.9.refs_1_, bf16[128,1024]{1,0:T(8,128)(2,1)} %get-tuple-element.10.refs_2_, ...), custom_call_target="tpu_custom_call" | custom-call | tf_op jit(solution)/shard_map/turn_results/pallas_call | solution.py:591
